TPU v7x, 32 devices: a whole 2x2x4 slice. The times are simulated.
32 devices in a mesh: feat: 2 (over y), row: 16 (over z, x, core).
Axes of the slice: x: 2, y: 2, z: 4, core: 2. Of those that a mesh axis runs over, the one named last changes fastest.
Arguments:
- bin_values: int32 [32768, 256], P('row', 'feat'), may hold values from 0 to 127
- leaf_ids: int32 [32768], P('row'), may hold values from 0 to 3
- treated: int32 [32768], P('row'), may hold values 0 or 1
- gradient: bfloat16 [32768], P('row'), may hold values from -6 to 6
- hessian: bfloat16 [32768], P('row'), may hold values from 0.099609375 to 2
Outputs:
- split_gain: float32 [4, 256, 128], P(None, ('feat', 'row'))
- best_gain: float32 [4], replicated
All inputs are finite; a program needn't handle non-finite values. No bound on the sum of `treated` on one device may be relied on, other than what follows from the above.
Results may differ from a plain program's by a relative error of at most 0.0003.
Values sent between devices are 32-bit elements; how exact they have to be, the bound alone decides.
No kernel may reach another device: no remote copies, remote signals or barrier semaphores. Data moves between devices by JAX's collectives and lax.ppermute only.
A program may use at most 64 MiB of HBM per device.

v0:
```python
import math

import jax
import jax.numpy as jnp
from jax import lax
from jax.sharding import PartitionSpec as P

BINS = 128
LEAVES = 4


def arm_stats(leaf_ids, treated, gradient, hessian, leaf_count):
    chosen = treated.astype(jnp.bfloat16)
    others = (1 - treated).astype(jnp.bfloat16)
    columns = jnp.stack(
        [gradient * chosen, hessian * chosen, gradient * others, hessian * others], axis=1
    )
    leaf_hot = (leaf_ids[:, None] == jnp.arange(leaf_count, dtype=jnp.int32)[None, :]).astype(
        jnp.bfloat16
    )
    return (columns[:, :, None] * leaf_hot[:, None, :]).reshape(leaf_ids.shape[0], 4 * leaf_count)


def node_score(totals, leaf_count):
    split_up = totals.reshape(totals.shape[0], 4, leaf_count, totals.shape[2])
    grad_t = split_up[:, 0]
    hess_t = split_up[:, 1]
    grad_c = split_up[:, 2]
    hess_c = split_up[:, 3]
    value_t = grad_t / (hess_t + 1.0)
    value_c = grad_c / (hess_c + 1.0)
    spread = value_t - value_c
    return grad_t * value_t + grad_c * value_c + (hess_t + hess_c) * spread * spread


def body(bin_values, leaf_ids, treated, gradient, hessian):
    row_count, feat_count = bin_values.shape
    bin_count = BINS
    leaf_count = LEAVES
    share_size = feat_count // lax.axis_size("row")
    stat_rows = arm_stats(leaf_ids, treated, gradient, hessian, leaf_count)
    bin_range = jnp.arange(bin_count, dtype=jnp.int32)

    def one_block(feat_block):
        one_hot = (feat_block[:, :, None] == bin_range[None, None, :]).astype(jnp.bfloat16)
        return jnp.einsum("rc,rfb->fcb", stat_rows, one_hot, preferred_element_type=jnp.float32)

    block_width = math.gcd(feat_count, 8)
    blocks = jnp.moveaxis(
        bin_values.reshape(row_count, feat_count // block_width, block_width), 1, 0
    )
    summed = lax.psum(
        lax.map(one_block, blocks).reshape(feat_count, 4 * leaf_count, bin_count), "row"
    )
    owned_rows = lax.dynamic_slice_in_dim(summed, lax.axis_index("row") * share_size, share_size, 0)
    ladder = (bin_range[:, None] <= bin_range[None, :]).astype(jnp.float32)
    left_sums = jnp.einsum("fcb,bk->fck", owned_rows, ladder, precision=lax.Precision.HIGHEST)
    parent_sums = left_sums[:, :, bin_count - 1 :]
    right_sums = parent_sums - left_sums
    gains_local = (
        node_score(left_sums, leaf_count)
        + node_score(right_sums, leaf_count)
        - node_score(parent_sums, leaf_count)
    )
    split_gain = jnp.transpose(gains_local, (1, 0, 2))
    best_gain = lax.pmax(jnp.max(gains_local, axis=(0, 2)), ("feat", "row"))
    return (split_gain, best_gain)


def solution(mesh):
    in_specs = (P("row", "feat"), P("row"), P("row"), P("row"), P("row"))
    out_specs = (P(None, ("feat", "row"), None), P())
    return jax.shard_map(body, mesh=mesh, in_specs=in_specs, out_specs=out_specs, check_vma=False)
```

profile of v0, /device:TPU:0, one launch (start us, length us, event | category | flops | bytes accessed | tf_op | source)
XLA Modules:
  0.0 212.4 jit_solution(4552845755185892554)
XLA Ops:
  7.2 0.0 all-reduce.2.cloned.1.call-start
  7.2 0.8 convert_multiply_fusion.1
  8.1 0.0 copy-start
  8.1 1.6 copy.17
  9.6 0.0 copy-done
  9.7 58.0 %while.11 = (s32[]{:T(128)}, f32[16,8,16,128]{3,2,1,0:T(8,128)}, s32[16,2048,8]{1,2,0:T(8,128)S(1)}, bf16[2048,4]{0,1:T(4,128)(2,1)S(1)}, bf16[2048,4]{0,1:T(4,128)(2,1)S(1)}, /*index=5*/s32[]{:T(128)}) while((s32[]{:T(128)}, f32[16,8,16,128]{3,2,1,0:T(8,128)}, s32[16,2048,8]{1,2,0:T(8,128)S(1)}, bf16[2048,4]{0,1:T(4,128)(2,1)S(1)}, ...), condition=%wide.region_1.2_spmd.clone, body=%wide.region_0.1_spmd.clone.sunk | while | flops 69238784 | bytes 557641 | solution.py:53
  9.8 3.6 %fusion.29 = f32[16,8,16,128]{3,2,1,0:T(8,128)} fusion(f32[16,8,16,128]{3,2,1,0:T(8,128)} %get-tuple-element.115, s32[]{:T(128)} %get-tuple-element.114, bf16[2048,16,1]{0,1,2:T(8,128)(2,1)S(1)} %reshape.134, s32[2048,8]{0,1:T(8,128)S(1)} %dynamic-slice_bitcast_fusion.2), kind=kOutput, calls=%fused_computation.6.clone.1 | convolution fusion | flops 69206016 | bytes 197120 | tf_op jit(solution)/shard_map/while/body/eval_jaxpr/rc,rfb->fcb/dot_general | solution.py:46
  13.5 3.5 %fusion.29 = f32[16,8,16,128]{3,2,1,0:T(8,128)} fusion(f32[16,8,16,128]{3,2,1,0:T(8,128)} %get-tuple-element.115, s32[]{:T(128)} %get-tuple-element.114, bf16[2048,16,1]{0,1,2:T(8,128)(2,1)S(1)} %reshape.134, s32[2048,8]{0,1:T(8,128)S(1)} %dynamic-slice_bitcast_fusion.2), kind=kOutput, calls=%fused_computation.6.clone.1 | convolution fusion | flops 69206016 | bytes 197120 | tf_op jit(solution)/shard_map/while/body/eval_jaxpr/rc,rfb->fcb/dot_general | solution.py:46
  17.1 3.6 %fusion.29 = f32[16,8,16,128]{3,2,1,0:T(8,128)} fusion(f32[16,8,16,128]{3,2,1,0:T(8,128)} %get-tuple-element.115, s32[]{:T(128)} %get-tuple-element.114, bf16[2048,16,1]{0,1,2:T(8,128)(2,1)S(1)} %reshape.134, s32[2048,8]{0,1:T(8,128)S(1)} %dynamic-slice_bitcast_fusion.2), kind=kOutput, calls=%fused_computation.6.clone.1 | convolution fusion | flops 69206016 | bytes 197120 | tf_op jit(solution)/shard_map/while/body/eval_jaxpr/rc,rfb->fcb/dot_general | solution.py:46
  20.7 3.5 %fusion.29 = f32[16,8,16,128]{3,2,1,0:T(8,128)} fusion(f32[16,8,16,128]{3,2,1,0:T(8,128)} %get-tuple-element.115, s32[]{:T(128)} %get-tuple-element.114, bf16[2048,16,1]{0,1,2:T(8,128)(2,1)S(1)} %reshape.134, s32[2048,8]{0,1:T(8,128)S(1)} %dynamic-slice_bitcast_fusion.2), kind=kOutput, calls=%fused_computation.6.clone.1 | convolution fusion | flops 69206016 | bytes 197120 | tf_op jit(solution)/shard_map/while/body/eval_jaxpr/rc,rfb->fcb/dot_general | solution.py:46
  24.3 3.6 %fusion.29 = f32[16,8,16,128]{3,2,1,0:T(8,128)} fusion(f32[16,8,16,128]{3,2,1,0:T(8,128)} %get-tuple-element.115, s32[]{:T(128)} %get-tuple-element.114, bf16[2048,16,1]{0,1,2:T(8,128)(2,1)S(1)} %reshape.134, s32[2048,8]{0,1:T(8,128)S(1)} %dynamic-slice_bitcast_fusion.2), kind=kOutput, calls=%fused_computation.6.clone.1 | convolution fusion | flops 69206016 | bytes 197120 | tf_op jit(solution)/shard_map/while/body/eval_jaxpr/rc,rfb->fcb/dot_general | solution.py:46
  28.0 3.5 %fusion.29 = f32[16,8,16,128]{3,2,1,0:T(8,128)} fusion(f32[16,8,16,128]{3,2,1,0:T(8,128)} %get-tuple-element.115, s32[]{:T(128)} %get-tuple-element.114, bf16[2048,16,1]{0,1,2:T(8,128)(2,1)S(1)} %reshape.134, s32[2048,8]{0,1:T(8,128)S(1)} %dynamic-slice_bitcast_fusion.2), kind=kOutput, calls=%fused_computation.6.clone.1 | convolution fusion | flops 69206016 | bytes 197120 | tf_op jit(solution)/shard_map/while/body/eval_jaxpr/rc,rfb->fcb/dot_general | solution.py:46
  31.6 3.6 %fusion.29 = f32[16,8,16,128]{3,2,1,0:T(8,128)} fusion(f32[16,8,16,128]{3,2,1,0:T(8,128)} %get-tuple-element.115, s32[]{:T(128)} %get-tuple-element.114, bf16[2048,16,1]{0,1,2:T(8,128)(2,1)S(1)} %reshape.134, s32[2048,8]{0,1:T(8,128)S(1)} %dynamic-slice_bitcast_fusion.2), kind=kOutput, calls=%fused_computation.6.clone.1 | convolution fusion | flops 69206016 | bytes 197120 | tf_op jit(solution)/shard_map/while/body/eval_jaxpr/rc,rfb->fcb/dot_general | solution.py:46
  35.2 3.6 %fusion.29 = f32[16,8,16,128]{3,2,1,0:T(8,128)} fusion(f32[16,8,16,128]{3,2,1,0:T(8,128)} %get-tuple-element.115, s32[]{:T(128)} %get-tuple-element.114, bf16[2048,16,1]{0,1,2:T(8,128)(2,1)S(1)} %reshape.134, s32[2048,8]{0,1:T(8,128)S(1)} %dynamic-slice_bitcast_fusion.2), kind=kOutput, calls=%fused_computation.6.clone.1 | convolution fusion | flops 69206016 | bytes 197120 | tf_op jit(solution)/shard_map/while/body/eval_jaxpr/rc,rfb->fcb/dot_general | solution.py:46
  38.8 3.5 %fusion.29 = f32[16,8,16,128]{3,2,1,0:T(8,128)} fusion(f32[16,8,16,128]{3,2,1,0:T(8,128)} %get-tuple-element.115, s32[]{:T(128)} %get-tuple-element.114, bf16[2048,16,1]{0,1,2:T(8,128)(2,1)S(1)} %reshape.134, s32[2048,8]{0,1:T(8,128)S(1)} %dynamic-slice_bitcast_fusion.2), kind=kOutput, calls=%fused_computation.6.clone.1 | convolution fusion | flops 69206016 | bytes 197120 | tf_op jit(solution)/shard_map/while/body/eval_jaxpr/rc,rfb->fcb/dot_general | solution.py:46
  42.5 3.6 %fusion.29 = f32[16,8,16,128]{3,2,1,0:T(8,128)} fusion(f32[16,8,16,128]{3,2,1,0:T(8,128)} %get-tuple-element.115, s32[]{:T(128)} %get-tuple-element.114, bf16[2048,16,1]{0,1,2:T(8,128)(2,1)S(1)} %reshape.134, s32[2048,8]{0,1:T(8,128)S(1)} %dynamic-slice_bitcast_fusion.2), kind=kOutput, calls=%fused_computation.6.clone.1 | convolution fusion | flops 69206016 | bytes 197120 | tf_op jit(solution)/shard_map/while/body/eval_jaxpr/rc,rfb->fcb/dot_general | solution.py:46
  46.1 3.5 %fusion.29 = f32[16,8,16,128]{3,2,1,0:T(8,128)} fusion(f32[16,8,16,128]{3,2,1,0:T(8,128)} %get-tuple-element.115, s32[]{:T(128)} %get-tuple-element.114, bf16[2048,16,1]{0,1,2:T(8,128)(2,1)S(1)} %reshape.134, s32[2048,8]{0,1:T(8,128)S(1)} %dynamic-slice_bitcast_fusion.2), kind=kOutput, calls=%fused_computation.6.clone.1 | convolution fusion | flops 69206016 | bytes 197120 | tf_op jit(solution)/shard_map/while/body/eval_jaxpr/rc,rfb->fcb/dot_general | solution.py:46
  49.7 3.6 %fusion.29 = f32[16,8,16,128]{3,2,1,0:T(8,128)} fusion(f32[16,8,16,128]{3,2,1,0:T(8,128)} %get-tuple-element.115, s32[]{:T(128)} %get-tuple-element.114, bf16[2048,16,1]{0,1,2:T(8,128)(2,1)S(1)} %reshape.134, s32[2048,8]{0,1:T(8,128)S(1)} %dynamic-slice_bitcast_fusion.2), kind=kOutput, calls=%fused_computation.6.clone.1 | convolution fusion | flops 69206016 | bytes 197120 | tf_op jit(solution)/shard_map/while/body/eval_jaxpr/rc,rfb->fcb/dot_general | solution.py:46
  53.3 3.6 %fusion.29 = f32[16,8,16,128]{3,2,1,0:T(8,128)} fusion(f32[16,8,16,128]{3,2,1,0:T(8,128)} %get-tuple-element.115, s32[]{:T(128)} %get-tuple-element.114, bf16[2048,16,1]{0,1,2:T(8,128)(2,1)S(1)} %reshape.134, s32[2048,8]{0,1:T(8,128)S(1)} %dynamic-slice_bitcast_fusion.2), kind=kOutput, calls=%fused_computation.6.clone.1 | convolution fusion | flops 69206016 | bytes 197120 | tf_op jit(solution)/shard_map/while/body/eval_jaxpr/rc,rfb->fcb/dot_general | solution.py:46
  57.0 3.6 %fusion.29 = f32[16,8,16,128]{3,2,1,0:T(8,128)} fusion(f32[16,8,16,128]{3,2,1,0:T(8,128)} %get-tuple-element.115, s32[]{:T(128)} %get-tuple-element.114, bf16[2048,16,1]{0,1,2:T(8,128)(2,1)S(1)} %reshape.134, s32[2048,8]{0,1:T(8,128)S(1)} %dynamic-slice_bitcast_fusion.2), kind=kOutput, calls=%fused_computation.6.clone.1 | convolution fusion | flops 69206016 | bytes 197120 | tf_op jit(solution)/shard_map/while/body/eval_jaxpr/rc,rfb->fcb/dot_general | solution.py:46
  60.6 3.5 %fusion.29 = f32[16,8,16,128]{3,2,1,0:T(8,128)} fusion(f32[16,8,16,128]{3,2,1,0:T(8,128)} %get-tuple-element.115, s32[]{:T(128)} %get-tuple-element.114, bf16[2048,16,1]{0,1,2:T(8,128)(2,1)S(1)} %reshape.134, s32[2048,8]{0,1:T(8,128)S(1)} %dynamic-slice_bitcast_fusion.2), kind=kOutput, calls=%fused_computation.6.clone.1 | convolution fusion | flops 69206016 | bytes 197120 | tf_op jit(solution)/shard_map/while/body/eval_jaxpr/rc,rfb->fcb/dot_general | solution.py:46
  64.2 3.6 %fusion.29 = f32[16,8,16,128]{3,2,1,0:T(8,128)} fusion(f32[16,8,16,128]{3,2,1,0:T(8,128)} %get-tuple-element.115, s32[]{:T(128)} %get-tuple-element.114, bf16[2048,16,1]{0,1,2:T(8,128)(2,1)S(1)} %reshape.134, s32[2048,8]{0,1:T(8,128)S(1)} %dynamic-slice_bitcast_fusion.2), kind=kOutput, calls=%fused_computation.6.clone.1 | convolution fusion | flops 69206016 | bytes 197120 | tf_op jit(solution)/shard_map/while/body/eval_jaxpr/rc,rfb->fcb/dot_general | solution.py:46
  67.8 0.0 all-reduce.2.cloned.1.call-update
  67.8 96.1 %all-reduce.2.cloned.1.call-done = f32[128,16,128]{2,1,0:T(8,128)} async-done(((f32[128,16,128]{2,1,0:T(8,128)}), f32[128,16,128]{2,1,0:T(8,128)}) %all-reduce.2.cloned.1.call-update) | async-done | bytes 1048592 | tf_op jit(solution)/shard_map/psum | solution.py:52
  163.9 1.0 fusion.8
  164.9 0.2 slice_reduce_fusion
  165.1 0.1 broadcast_subtract_fusion
  165.2 0.2 copy.26
  165.4 0.7 fusion.21
  166.1 39.4 %pmax.7 = f32[4]{0:T(128)} all-reduce(f32[4]{0:T(128)S(1)} %get-tuple-element.55), channel_id=1, replica_groups=mesh['feat'=2,'row'=16] {'feat','row'}, use_global_device_ids=true, to_apply=%region_4.5 | all-reduce | flops 4 | bytes 32 | tf_op jit(solution)/shard_map/pmax | solution.py:66
  (57 shorter events, 1.2 us)
Async XLA Ops:
  7.2 156.7 %all-reduce.2.cloned.1.call-start = ((), (), s32[]{:S(2)}) async-start(), calls=%async_computation | async-start | bytes 2097152 | tf_op jit(solution)/shard_map/psum | solution.py:52
  8.1 1.6 copy-start
Sparse Core Ops, SparseCore 0:
  67.9 95.9 all-reduce.1
where the time goes:
time: 213 us; the launch traced here: 212 us
  waiting for transfers between devices  96.1 us (45%)
  matrix products  57.8 us (27%)
  blocking collectives  39.4 us (18%)
  between operations  14.1 us (7%)
  local copies, waits for them, and re-layouts  2.4 us (1%)
  other arithmetic  2.25 us (1%)
    psum x1, waiting for transfers between devices, body(): lax.psum(lax.map(one_block, blocks).reshape(feat_count, 4 * leaf_count, b...  96.1 us
    dot_general x16, matrix products, one_block(): jnp.einsum('rc,rfb->fcb', stat_rows, one_hot, preferred_element_type=jnp....  56.8 us
    pmax x1, blocking collectives, body(): best_gain = lax.pmax(jnp.max(gains_local, axis=(0, 2)), ('feat', 'row'))  39.4 us
  transfers between devices with their start and end apart: 1, of which 1 were waited for; matrix products, arithmetic and copies ran while one was open for 0% of the time, Pallas kernels for 0%

commit v1 on v0

v1 whole, which is shorter than its diff:
```python
import functools

import jax
import jax.numpy as jnp
from jax import lax
from jax.experimental import pallas as pl
from jax.experimental.pallas import tpu as pltpu
from jax.sharding import PartitionSpec as P

BINS = 128
LEAVES = 4
HALF = BINS // 2
STATS = 4 * LEAVES
PACK = 16
NT = (((1,), (1,)), ((), ()))
DEPTH = 256


def reversed_bits(value, bits):
    out = 0
    for i in range(bits):
        out = out + (((value >> i) & 1) << (bits - 1 - i))
    return out


def slot_of(position, kind, bits):
    if kind == "core":
        return reversed_bits(position, bits - 1) * 2 + 1
    if kind == "far":
        return (reversed_bits(position, bits - 2) * 2 + 1) * 2
    return reversed_bits(position, bits - 2) * 4


def stats_of(leaf, treated, gradient, hessian, stats_ref):
    row = lax.broadcasted_iota(jnp.int32, (STATS, 128), 0)
    stat, own_leaf = row // LEAVES, row % LEAVES
    grad, hess = gradient.astype(jnp.float32), hessian.astype(jnp.float32)
    for i in range(leaf.shape[0]):
        wide = lambda x: jnp.broadcast_to(x[i : i + 1], (STATS, 128))
        value = jnp.where(stat % 2 == 0, wide(grad), wide(hess))
        ok = (wide(leaf) == own_leaf) & ((wide(treated) == 1) == (stat < 2))
        stats_ref[:, i * 128 : (i + 1) * 128] = jnp.where(ok, value, 0.0).astype(jnp.bfloat16)


def left_sums_of(me, kind, bits, share, high_ref, low_ref, stats_ref, out_ref):
    rows = high_ref.shape[1]
    steps = lax.broadcasted_iota(jnp.int32, (PACK, DEPTH), 0).astype(jnp.float32).astype(jnp.bfloat16)

    def group(g, carry):
        feats = []
        for j in range(4):
            p = g * 4 + j
            feats.append((me ^ slot_of(p // share, kind, bits)) * share + p % share)
        high = [high_ref[pl.ds(f, 1), :] for f in feats]
        low = [low_ref[pl.ds(f, 1), :] for f in feats]
        total = jnp.zeros((5 * STATS, 4 * HALF), jnp.float32)
        for k in range(rows // DEPTH):
            span = slice(k * DEPTH, (k + 1) * DEPTH)
            left = [stats_ref[:, span]]
            ladder = []
            for j in range(4):
                wide = jnp.broadcast_to(low[j][:, span], (PACK, DEPTH)).astype(jnp.bfloat16)
                for q in range(HALF // PACK):
                    reached = wide <= steps + jnp.bfloat16(PACK * q)
                    ladder.append(jnp.where(reached, jnp.bfloat16(1), jnp.bfloat16(0)))
                left.append(left[0] * jnp.broadcast_to(high[j][:, span], (STATS, DEPTH)).astype(jnp.bfloat16))
            total += lax.dot_general(
                jnp.concatenate(left, 0), jnp.concatenate(ladder, 0), NT, preferred_element_type=jnp.float32
            )
        for j in range(4):
            columns = slice(HALF * j, HALF * (j + 1))
            upper = total[STATS * (j + 1) : STATS * (j + 2), columns]
            lower = total[:STATS, columns] - upper
            out_ref[g * 4 + j] = jnp.concatenate([lower, lower[:, HALF - 1 :] + upper], 1)
        return carry

    lax.fori_loop(0, out_ref.shape[0] // 4, group, 0, unroll=2)


def first_kernel(bits, share, bins, leaf, treated, gradient, hessian, high_ref, low_ref, stats_ref, out_ref, *scratch):
    held, sems = scratch[:-1], scratch[-1]
    copies = [
        pltpu.make_async_copy(src, dst, sems.at[i])
        for i, (src, dst) in enumerate(zip((leaf, treated, gradient, hessian, bins), held))
    ]
    for copy in copies:
        copy.start()
    for copy in copies[:4]:
        copy.wait()
    stats_of(held[0][...], held[1][...], held[2][...], held[3][...], stats_ref)
    copies[4].wait()
    turned = held[4][...].T
    high_ref[...] = (turned // HALF).astype(jnp.float32)
    low_ref[...] = (turned % HALF).astype(jnp.float32)
    left_sums_of(lax.axis_index("row"), "core", bits, share, high_ref, low_ref, stats_ref, out_ref)


def next_kernel(kind, bits, share, high_ref, low_ref, stats_ref, out_ref):
    left_sums_of(lax.axis_index("row"), kind, bits, share, high_ref, low_ref, stats_ref, out_ref)


def score_of(grad_t, hess_t, grad_c, hess_c):
    value_t = grad_t / (hess_t + 1.0)
    value_c = grad_c / (hess_c + 1.0)
    spread = value_t - value_c
    return grad_t * value_t + grad_c * value_c + (hess_t + hess_c) * spread * spread


def gain_kernel(kept_ref, came_ref, gain_ref, most_ref):
    lane = lax.broadcasted_iota(jnp.int32, most_ref.shape, 1)
    most = jnp.zeros(most_ref.shape, jnp.float32)
    for leaf in range(LEAVES):
        left = [
            kept_ref[:, s * LEAVES + leaf, :] + came_ref[:, s * LEAVES + leaf, :] for s in range(4)
        ]
        parent = [jnp.broadcast_to(x[:, BINS - 1 :], x.shape) for x in left]
        right = [p - x for p, x in zip(parent, left)]
        gain = score_of(*left) + score_of(*right) - score_of(*parent)
        gain_ref[leaf] = gain
        most = jnp.where(lane == leaf, jnp.max(gain), most)
    most_ref[...] = most


VMEM = pl.BlockSpec(memory_space=pltpu.VMEM)
ANY = pl.BlockSpec(memory_space=pl.ANY)
ROOM = pltpu.CompilerParams(vmem_limit_bytes=32 * 2**20)


def body(devices, bin_values, leaf_ids, treated, gradient, hessian):
    rows, feats = bin_values.shape
    ring = lax.axis_size("row")
    bits = ring.bit_length() - 1
    share = feats // ring
    f32 = jnp.float32
    small = (rows // 128, 128)

    def work(count):
        return pl.CostEstimate(
            flops=2 * rows * count * BINS * STATS * 2, bytes_accessed=rows * count * 8, transcendentals=0
        )

    high, low, stats, core_part = pl.pallas_call(
        functools.partial(first_kernel, bits, share),
        out_shape=(
            jax.ShapeDtypeStruct((feats, rows), f32),
            jax.ShapeDtypeStruct((feats, rows), f32),
            jax.ShapeDtypeStruct((STATS, rows), jnp.bfloat16),
            jax.ShapeDtypeStruct((feats // 2, STATS, BINS), f32),
        ),
        in_specs=[ANY] * 5,
        out_specs=(VMEM,) * 4,
        scratch_shapes=[
            pltpu.VMEM(small, jnp.int32),
            pltpu.VMEM(small, jnp.int32),
            pltpu.VMEM(small, jnp.bfloat16),
            pltpu.VMEM(small, jnp.bfloat16),
            pltpu.VMEM((rows, feats), jnp.int32),
            pltpu.SemaphoreType.DMA((5,)),
        ],
        compiler_params=ROOM,
        cost_estimate=work(feats // 2),
        name="stats_and_core_part",
    )(bin_values, *(x.reshape(small) for x in (leaf_ids, treated, gradient, hessian)))

    def part(kind):
        return pl.pallas_call(
            functools.partial(next_kernel, kind, bits, share),
            out_shape=jax.ShapeDtypeStruct((feats // 4, STATS, BINS), f32),
            in_specs=[VMEM] * 3,
            out_specs=VMEM,
            compiler_params=ROOM,
            cost_estimate=work(feats // 4),
            name=kind + "_part",
        )(high, low, stats)

    def swap(x, bit):
        return lax.ppermute(x, "row", [(i, i ^ bit) for i in range(ring)])

    core_came = swap(core_part, 1)
    far = part("far")
    near = part("near")
    half = feats // 4
    far_came = swap(far + core_came[half:], 2)
    kept = near + core_came[:half]
    came = far_came
    for stage in range(2, bits):
        half = half // 2
        sent = kept[half:] + came[half:]
        kept = kept[:half] + came[:half]
        came = swap(sent, 1 << stage)

    split_gain, most = pl.pallas_call(
        gain_kernel,
        out_shape=(
            jax.ShapeDtypeStruct((LEAVES, share, BINS), f32),
            jax.ShapeDtypeStruct((devices, BINS), f32),
        ),
        in_specs=[VMEM] * 2,
        out_specs=(VMEM,) * 2,
        name="gains",
    )(kept, came)
    best = lax.all_to_all(most, ("feat", "row"), 0, 0, tiled=True)
    return split_gain, jnp.max(best, axis=0)[:LEAVES]


def solution(mesh):
    in_specs = (P("row", "feat"), P("row"), P("row"), P("row"), P("row"))
    out_specs = (P(None, ("feat", "row"), None), P())
    return jax.shard_map(
        functools.partial(body, mesh.size), mesh=mesh, in_specs=in_specs, out_specs=out_specs, check_vma=False
    )
```

time: 213 us -> 59 us (0.28)
  waiting for transfers between devices: 96.1 us -> 13 us
  matrix products: 57.8 us -> 0 us
  blocking collectives: 39.4 us -> 13.6 us
  Pallas kernels: 0 us -> 17.8 us
  between operations: 14.1 us -> 0.68 us
  starting transfers between devices: 0.04 us -> 7.62 us
  local copies, waits for them, and re-layouts: 2.4 us -> 4.6 us
    psum x1 -> x0, waiting for transfers between devices: 96.1 us -> none  [body(): lax.psum(lax.map(one_block, blocks).reshape(feat_count, 4 * leaf_count, b...]
    dot_general x17 -> x0, matrix products: 57.8 us -> none  [the longest x16 56.8 us: one_block(): jnp.einsum('rc,rfb->fcb', stat_rows, one_hot, preferred_element_type=jnp....]
    pmax x1 -> x0, blocking collectives: 39.4 us -> none  [body(): best_gain = lax.pmax(jnp.max(gains_local, axis=(0, 2)), ('feat', 'row'))]
    pallas_call x0 -> x4, Pallas kernels: none -> 17.8 us  [the longest x1 8.53 us: body(): pl.pallas_call(functools.partial(first_kernel, bits, share), out_shape=(j...]
    all_to_all x0 -> x1, blocking collectives: none -> 13.6 us  [body(): best = lax.all_to_all(most, ('feat', 'row'), 0, 0, tiled=True)]
    ppermute x0 -> x4, waiting for transfers between devices: none -> 13 us  [swap(): return lax.ppermute(x, 'row', [(i, i ^ bit) for i in range(ring)])]
    ppermute x0 -> x4, starting transfers between devices: none -> 7.62 us  [swap(): return lax.ppermute(x, 'row', [(i, i ^ bit) for i in range(ring)])]
    unnamed x3 -> x12, local copies, waits for them, and re-layouts: 1.57 us -> 4.6 us
  transfers between devices with their start and end apart: 1 -> 4, of which waited for: 1 -> 3; matrix products, arithmetic and copies ran while one was open for 0% -> 0% of each run, Pallas kernels for 0% -> 13%
where the time goes in v1:
time: 59 us; the launch traced here: 58.6 us
  Pallas kernels  17.8 us (30%)
  blocking collectives  13.6 us (23%)
  waiting for transfers between devices  13 us (22%)
  starting transfers between devices  7.62 us (13%)
  local copies, waits for them, and re-layouts  4.6 us (8%)
  other arithmetic  1.31 us (2%)
  between operations  0.68 us (1%)
    all_to_all x1, blocking collectives, body(): best = lax.all_to_all(most, ('feat', 'row'), 0, 0, tiled=True)  13.6 us
    ppermute x4, waiting for transfers between devices, swap(): return lax.ppermute(x, 'row', [(i, i ^ bit) for i in range(ring)])  13 us
    pallas_call x1, Pallas kernels, body(): pl.pallas_call(functools.partial(first_kernel, bits, share), out_shape=(j...  8.53 us
    ppermute x4, starting transfers between devices, swap(): return lax.ppermute(x, 'row', [(i, i ^ bit) for i in range(ring)])  7.62 us
    pallas_call x2, Pallas kernels, part(): pl.pallas_call(functools.partial(next_kernel, kind, bits, share), out_sha...  7.39 us
    unnamed x12, local copies, waits for them, and re-layouts  4.6 us
    pallas_call x1, Pallas kernels, body(): pl.pallas_call(gain_kernel, out_shape=(jax.ShapeDtypeStruct((LEAVES, shar...  1.91 us
  transfers between devices with their start and end apart: 4, of which 3 were waited for; matrix products, arithmetic and copies ran while one was open for 0% of the time, Pallas kernels for 13%

profile of v1, /device:TPU:0, one launch (start us, length us, event | category | flops | bytes accessed | tf_op | source)
XLA Modules:
  0.0 58.6 jit_solution(10987743208537205662)
XLA Ops:
  0.6 0.0 copy-start.3
  0.6 0.7 %copy-done.3 = bf16[2048]{0:T(1024)(128)(2,1)S(1)} copy-done((bf16[2048]{0:T(1024)(128)(2,1)S(1)}, bf16[2048]{0:T(1024)(128)(2,1)}, u32[]{:S(2)}) %copy-start.3) | copy-done | bytes 4120
  1.3 0.0 copy-start
  1.3 1.2 %copy-done = s32[2048,128]{1,0:T(8,128)S(1)} copy-done((s32[2048,128]{1,0:T(8,128)S(1)}, s32[2048,128]{1,0:T(8,128)}, u32[]{:S(2)}) %copy-start) | copy-done | bytes 1048600
  2.5 0.0 copy-start.1
  2.5 0.7 %copy-done.1 = s32[2048]{0:T(1024)S(1)} copy-done((s32[2048]{0:T(1024)S(1)}, s32[2048]{0:T(1024)}, u32[]{:S(2)}) %copy-start.1) | copy-done | bytes 8216
  3.2 0.0 copy-start.2
  3.2 0.7 %copy-done.2 = s32[2048]{0:T(1024)S(1)} copy-done((s32[2048]{0:T(1024)S(1)}, s32[2048]{0:T(1024)}, u32[]{:S(2)}) %copy-start.2) | copy-done | bytes 8216
  3.9 0.0 copy-start.4
  3.9 0.7 %copy-done.4 = bf16[2048]{0:T(1024)(128)(2,1)S(1)} copy-done((bf16[2048]{0:T(1024)(128)(2,1)S(1)}, bf16[2048]{0:T(1024)(128)(2,1)}, u32[]{:S(2)}) %copy-start.4) | copy-done | bytes 4120
  4.6 8.5 %stats_and_core_part.1 = (f32[128,2048]{1,0:T(8,128)S(1)}, f32[128,2048]{1,0:T(8,128)S(1)}, bf16[16,2048]{1,0:T(8,128)(2,1)S(1)}, f32[64,16,128]{2,1,0:T(8,128)S(1)}) custom-call(s32[2048,128]{1,0:T(8,128)S(1)} %copy-done, s32[16,128]{1,0:T(8,128)S(1)} %bitcast.8, s32[16,128]{1,0:T(8,128)S(1)} %bitcast.9, bf16[16,128]{1,0:T(8,128)(2,1)S(1)} %bitcast.10, ...), custom_call_target="tpu_custom_call" | custom-call | flops 1073741824 | bytes 1048576 | tf_op jit(solution)/shard_map/stats_and_core_part/pallas_call | solution.py:142
  13.2 0.5 collective-permute-start
  13.7 3.7 %far_part.1 = f32[32,16,128]{2,1,0:T(8,128)S(1)} custom-call(f32[128,2048]{1,0:T(8,128)S(1)} %get-tuple-element.8.high_ref, f32[128,2048]{1,0:T(8,128)S(1)} %get-tuple-element.9.low_ref, bf16[16,2048]{1,0:T(8,128)(2,1)S(1)} %get-tuple-element.10.stats_ref), custom_call_target="tpu_custom_call" | custom-call | flops 536870912 | bytes 524288 | tf_op jit(solution)/shard_map/far_part/pallas_call | solution.py:166
  17.4 3.7 %near_part.1 = f32[32,16,128]{2,1,0:T(8,128)S(1)} custom-call(f32[128,2048]{1,0:T(8,128)S(1)} %get-tuple-element.8.high_ref, f32[128,2048]{1,0:T(8,128)S(1)} %get-tuple-element.9.low_ref, bf16[16,2048]{1,0:T(8,128)(2,1)S(1)} %get-tuple-element.10.stats_ref), custom_call_target="tpu_custom_call" | custom-call | flops 536870912 | bytes 524288 | tf_op jit(solution)/shard_map/near_part/pallas_call | solution.py:166
  21.1 0.0 collective-permute-done
  21.1 0.1 slice_add_fusion.1
  21.2 2.6 %collective-permute-start.1 = (f32[32,16,128]{2,1,0:T(8,128)S(1)}, f32[32,16,128]{2,1,0:T(8,128)S(1)}, u32[]{:S(2)}, u32[]{:S(2)}) collective-permute-start(f32[32,16,128]{2,1,0:T(8,128)S(1)} %get-tuple-element.17), channel_id=1, source_target_pairs={{0,2},{1,3},{2,0},{3,1},{4,6},{5,7},{6,4},{7,5},{8,10},{9,11},{10,... | collective-permute-start | bytes 786440 | tf_op jit(solution)/shard_map/ppermute | solution.py:177
  23.7 7.0 %collective-permute-done.1 = f32[32,16,128]{2,1,0:T(8,128)S(1)} collective-permute-done((f32[32,16,128]{2,1,0:T(8,128)S(1)}, f32[32,16,128]{2,1,0:T(8,128)S(1)}, u32[]{:S(2)}, u32[]{:S(2)}) %collective-permute-start.1) | collective-permute-done | bytes 262176 | tf_op jit(solution)/shard_map/ppermute | solution.py:177
  30.7 1.9 %collective-permute-start.2 = (f32[16,16,128]{2,1,0:T(8,128)S(1)}, f32[16,16,128]{2,1,0:T(8,128)S(1)}, u32[]{:S(2)}, u32[]{:S(2)}) collective-permute-start(f32[16,16,128]{2,1,0:T(8,128)S(1)} %get-tuple-element.15), channel_id=1, source_target_pairs={{0,4},{1,5},{2,6},{3,7},{4,0},{5,1},{6,2},{7,3},{8,12},{9,13},{10,... | collective-permute-start | bytes 393224 | tf_op jit(solution)/shard_map/ppermute | solution.py:177
  32.6 3.5 %collective-permute-done.2 = f32[16,16,128]{2,1,0:T(8,128)S(1)} collective-permute-done((f32[16,16,128]{2,1,0:T(8,128)S(1)}, f32[16,16,128]{2,1,0:T(8,128)S(1)}, u32[]{:S(2)}, u32[]{:S(2)}) %collective-permute-start.2) | collective-permute-done | bytes 131104 | tf_op jit(solution)/shard_map/ppermute | solution.py:177
  36.1 0.6 %slice_add_fusion.4 = (f32[8,16,128]{2,1,0:T(8,128)S(1)}, f32[8,16,128]{2,1,0:T(8,128)}) fusion(f32[16,16,128]{2,1,0:T(8,128)S(1)} %collective-permute-done.2, f32[16,16,128]{2,1,0:T(8,128)S(1)} %get-tuple-element.14), kind=kLoop, calls=%fused_computation.4 | loop fusion | flops 32768 | bytes 393216 | tf_op jit(solution)/shard_map/add | solution.py:188
  36.8 2.6 %collective-permute-start.3 = (f32[8,16,128]{2,1,0:T(8,128)S(1)}, f32[8,16,128]{2,1,0:T(8,128)S(1)}, u32[]{:S(2)}, u32[]{:S(2)}) collective-permute-start(f32[8,16,128]{2,1,0:T(8,128)S(1)} %get-tuple-element.18), channel_id=1, source_target_pairs={{0,8},{1,9},{2,10},{3,11},{4,12},{5,13},{6,14},{7,15},{8,0},{9,1},... | collective-permute-start | bytes 196616 | tf_op jit(solution)/shard_map/ppermute | solution.py:177
  39.4 2.5 %collective-permute-done.3.came_ref = f32[8,16,128]{2,1,0:T(8,128)S(1)} collective-permute-done((f32[8,16,128]{2,1,0:T(8,128)S(1)}, f32[8,16,128]{2,1,0:T(8,128)S(1)}, u32[]{:S(2)}, u32[]{:S(2)}) %collective-permute-start.3) | collective-permute-done | bytes 65568 | tf_op jit(solution)/shard_map/ppermute | solution.py:177
  41.9 0.0 copy-start.5
  41.9 0.6 %copy-done.5 = f32[8,16,128]{2,1,0:T(8,128)} copy-done((f32[8,16,128]{2,1,0:T(8,128)}, f32[8,16,128]{2,1,0:T(8,128)S(1)}, u32[]{:S(2)}) %copy-start.5) | copy-done | bytes 65560
  42.6 1.9 %gains.1 = (f32[4,8,128]{2,1,0:T(8,128)}, f32[32,128]{1,0:T(8,128)}) custom-call(f32[8,16,128]{2,1,0:T(8,128)} %get-tuple-element.19.kept_ref, f32[8,16,128]{2,1,0:T(8,128)} %copy-done.5), custom_call_target="tpu_custom_call" | custom-call | tf_op jit(solution)/shard_map/gains/pallas_call | solution.py:192
  44.5 13.6 %all_to_all.9 = f32[32,1,128]{2,1,0:T(1,128)S(1)} all-to-all(f32[32,1,128]{2,1,0:T(1,128)} %bitcast.12), channel_id=1, replica_groups=mesh['feat'=2,'row'=16] {'feat','row'}, dimensions={0} | all-to-all | bytes 32768 | tf_op jit(solution)/shard_map/all_to_all | solution.py:202
  58.1 0.6 reduce_max.9
  (1 shorter events, 0.0 us)
Async XLA Ops:
  0.6 0.7 %copy-start.3 = (bf16[2048]{0:T(1024)(128)(2,1)S(1)}, bf16[2048]{0:T(1024)(128)(2,1)}, u32[]{:S(2)}) copy-start(bf16[2048]{0:T(1024)(128)(2,1)} %param.8) | copy-start | bytes 12292
  1.3 1.2 %copy-start = (s32[2048,128]{1,0:T(8,128)S(1)}, s32[2048,128]{1,0:T(8,128)}, u32[]{:S(2)}) copy-start(s32[2048,128]{1,0:T(8,128)} %bins.1) | copy-start | bytes 3145732
  2.5 0.7 %copy-start.1 = (s32[2048]{0:T(1024)S(1)}, s32[2048]{0:T(1024)}, u32[]{:S(2)}) copy-start(s32[2048]{0:T(1024)} %param.6) | copy-start | bytes 24580
  3.2 0.7 %copy-start.2 = (s32[2048]{0:T(1024)S(1)}, s32[2048]{0:T(1024)}, u32[]{:S(2)}) copy-start(s32[2048]{0:T(1024)} %param.7) | copy-start | bytes 24580
  3.9 0.7 %copy-start.4 = (bf16[2048]{0:T(1024)(128)(2,1)S(1)}, bf16[2048]{0:T(1024)(128)(2,1)}, u32[]{:S(2)}) copy-start(bf16[2048]{0:T(1024)(128)(2,1)} %param.9) | copy-start | bytes 12292
  13.2 7.9 %collective-permute-start = (f32[64,16,128]{2,1,0:T(8,128)S(1)}, f32[64,16,128]{2,1,0:T(8,128)S(1)}, u32[]{:S(2)}, u32[]{:S(2)}) collective-permute-start(f32[64,16,128]{2,1,0:T(8,128)S(1)} %get-tuple-element.11), channel_id=1, source_target_pairs={{0,1},{1,0},{2,3},{3,2},{4,5},{5,4},{6,7},{7,6},{8,9},{9,8},{10,11... | collective-permute-start | bytes 1572872 | tf_op jit(solution)/shard_map/ppermute | solution.py:177
  21.2 9.5 %collective-permute-start.1 = (f32[32,16,128]{2,1,0:T(8,128)S(1)}, f32[32,16,128]{2,1,0:T(8,128)S(1)}, u32[]{:S(2)}, u32[]{:S(2)}) collective-permute-start(f32[32,16,128]{2,1,0:T(8,128)S(1)} %get-tuple-element.17), channel_id=1, source_target_pairs={{0,2},{1,3},{2,0},{3,1},{4,6},{5,7},{6,4},{7,5},{8,10},{9,11},{10,... | collective-permute-start | bytes 786440 | tf_op jit(solution)/shard_map/ppermute | solution.py:177
  30.7 5.4 %collective-permute-start.2 = (f32[16,16,128]{2,1,0:T(8,128)S(1)}, f32[16,16,128]{2,1,0:T(8,128)S(1)}, u32[]{:S(2)}, u32[]{:S(2)}) collective-permute-start(f32[16,16,128]{2,1,0:T(8,128)S(1)} %get-tuple-element.15), channel_id=1, source_target_pairs={{0,4},{1,5},{2,6},{3,7},{4,0},{5,1},{6,2},{7,3},{8,12},{9,13},{10,... | collective-permute-start | bytes 393224 | tf_op jit(solution)/shard_map/ppermute | solution.py:177
  36.8 5.2 %collective-permute-start.3 = (f32[8,16,128]{2,1,0:T(8,128)S(1)}, f32[8,16,128]{2,1,0:T(8,128)S(1)}, u32[]{:S(2)}, u32[]{:S(2)}) collective-permute-start(f32[8,16,128]{2,1,0:T(8,128)S(1)} %get-tuple-element.18), channel_id=1, source_target_pairs={{0,8},{1,9},{2,10},{3,11},{4,12},{5,13},{6,14},{7,15},{8,0},{9,1},... | collective-permute-start | bytes 196616 | tf_op jit(solution)/shard_map/ppermute | solution.py:177
  41.9 0.6 %copy-start.5 = (f32[8,16,128]{2,1,0:T(8,128)}, f32[8,16,128]{2,1,0:T(8,128)S(1)}, u32[]{:S(2)}) copy-start(f32[8,16,128]{2,1,0:T(8,128)S(1)} %collective-permute-done.3.came_ref) | copy-start | bytes 196612

commit v2 on v1

v2 whole, which is shorter than its diff:
```python
import functools

import jax
import jax.numpy as jnp
from jax import lax
from jax.experimental import pallas as pl
from jax.experimental.pallas import tpu as pltpu
from jax.sharding import PartitionSpec as P

BINS = 128
LEAVES = 4
STATS = 4 * LEAVES
PACK = 16
HIGH = 4
LOW = BINS // HIGH
GROUP = 8
DEPTH = 256
NT = (((1,), (1,)), ((), ()))
F32, BF16 = jnp.float32, jnp.bfloat16


def reversed_bits(value, bits):
    out = 0
    for i in range(bits):
        out = out + (((value >> i) & 1) << (bits - 1 - i))
    return out


def slot_of(position, far, other, bits):
    return reversed_bits(position, bits - 2) * 4 + 2 * far + other


def stats_of(leaf, treated, gradient, hessian, stats_ref):
    row = lax.broadcasted_iota(jnp.int32, (STATS, 128), 0)
    stat, own_leaf = row // LEAVES, row % LEAVES
    grad, hess = gradient.astype(F32), hessian.astype(F32)
    for i in range(leaf.shape[0]):
        wide = lambda x: jnp.broadcast_to(x[i : i + 1], (STATS, 128))
        value = jnp.where(stat % 2 == 0, wide(grad), wide(hess))
        ok = (wide(leaf) == own_leaf) & ((wide(treated) == 1) == (stat < 2))
        stats_ref[:, i * 128 : (i + 1) * 128] = jnp.where(ok, value, 0.0).astype(BF16)


def left_sums_of(me, far, other, bits, share, bins_ref, low_ref, stats_ref, out_ref):
    rows = bins_ref.shape[1]
    steps = lax.broadcasted_iota(jnp.int32, (PACK, DEPTH), 0).astype(F32).astype(BF16)
    one, zero = BF16(1), BF16(0)
    for g in range(out_ref.shape[0] // GROUP):
        feats = []
        for p in range(g * GROUP, (g + 1) * GROUP):
            feats.append((me ^ slot_of(p // share, far, other, bits)) * share + p % share)
        bins = [bins_ref[pl.ds(f, 1), :] for f in feats]
        low = [low_ref[pl.ds(f, 1), :] for f in feats]
        total = jnp.zeros((STATS * (1 + (HIGH - 1) * GROUP), LOW * GROUP), F32)
        for k in range(rows // DEPTH):
            span = slice(k * DEPTH, (k + 1) * DEPTH)
            stats = stats_ref[:, span]
            streamed, ladder = [stats], []
            for j in range(GROUP):
                wide = jnp.broadcast_to(low[j][:, span], (PACK, DEPTH)).astype(BF16)
                for q in range(LOW // PACK):
                    ladder.append(jnp.where(wide <= steps + BF16(PACK * q), one, zero))
                wide = jnp.broadcast_to(bins[j][:, span], (STATS, DEPTH)).astype(BF16)
                for q in range(1, HIGH):
                    streamed.append(jnp.where(wide >= BF16(LOW * q), stats, zero))
            total += lax.dot_general(
                jnp.concatenate(streamed, 0), jnp.concatenate(ladder, 0), NT, preferred_element_type=F32
            )
        for j in range(GROUP):
            columns = slice(LOW * j, LOW * (j + 1))
            reached = [total[:STATS, columns]]
            for q in range(1, HIGH):
                first = STATS * (1 + (HIGH - 1) * j + q - 1)
                reached.append(total[first : first + STATS, columns])
            pieces = []
            for q in range(HIGH):
                piece = reached[q]
                if q + 1 < HIGH:
                    piece = piece - reached[q + 1]
                if q:
                    piece = piece + (reached[0][:, LOW - 1 :] - reached[q][:, LOW - 1 :])
                pieces.append(piece)
            out_ref[g * GROUP + j] = jnp.concatenate(pieces, 1)


def first_kernel(bits, share, bins, leaf, treated, gradient, hessian, bins_ref, low_ref, stats_ref, out_ref, *scratch):
    held, sems = scratch[:-1], scratch[-1]
    copies = [
        pltpu.make_async_copy(src, dst, sems.at[i])
        for i, (src, dst) in enumerate(zip((bins, leaf, treated, gradient, hessian), held))
    ]
    for copy in copies:
        copy.start()
    for copy in copies[1:]:
        copy.wait()
    stats_of(*(ref[...] for ref in held[1:]), stats_ref)
    copies[0].wait()
    turned = held[0][...].T
    bins_ref[...] = turned.astype(F32)
    low_ref[...] = (turned % LOW).astype(F32)
    left_sums_of(lax.axis_index("row"), 1, 1, bits, share, bins_ref, low_ref, stats_ref, out_ref)


def next_kernel(far, other, bits, share, bins_ref, low_ref, stats_ref, after_ref, out_ref):
    left_sums_of(lax.axis_index("row"), far, other, bits, share, bins_ref, low_ref, stats_ref, out_ref)


def score_of(grad_t, hess_t, grad_c, hess_c):
    value_t = grad_t / (hess_t + 1.0)
    value_c = grad_c / (hess_c + 1.0)
    spread = value_t - value_c
    return grad_t * value_t + grad_c * value_c + (hess_t + hess_c) * spread * spread


def gain_kernel(kept_ref, came_ref, gain_ref, most_ref):
    tops = []
    for leaf in range(LEAVES):
        left = [kept_ref[:, s * LEAVES + leaf, :] + came_ref[:, s * LEAVES + leaf, :] for s in range(4)]
        parent = [jnp.broadcast_to(x[:, BINS - 1 :], x.shape) for x in left]
        right = [p - x for p, x in zip(parent, left)]
        gain = score_of(*left) + score_of(*right) - score_of(*parent)
        gain_ref[leaf] = gain
        tops.append(jnp.max(gain, axis=0, keepdims=True))
    top = jnp.max(jnp.concatenate(tops, 0), axis=1, keepdims=True)
    lane = lax.broadcasted_iota(jnp.int32, (LEAVES, BINS), 1)
    leaf = lax.broadcasted_iota(jnp.int32, (LEAVES, BINS), 0)
    line = jnp.sum(jnp.where(lane == leaf, top, 0.0), axis=0, keepdims=True)
    most_ref[...] = jnp.broadcast_to(line, most_ref.shape)


VMEM = pl.BlockSpec(memory_space=pltpu.VMEM)
HBM = pl.BlockSpec(memory_space=pltpu.HBM)
ANY = pl.BlockSpec(memory_space=pl.ANY)
ROOM = pltpu.CompilerParams(vmem_limit_bytes=32 * 2**20)


def body(devices, bin_values, leaf_ids, treated, gradient, hessian):
    rows, feats = bin_values.shape
    ring = lax.axis_size("row")
    bits = ring.bit_length() - 1
    share = feats // ring
    small = (rows // 128, 128)
    part = jax.ShapeDtypeStruct((feats // 4, STATS, BINS), F32)
    cost = pl.CostEstimate(
        flops=2 * rows * feats // 4 * BINS * STATS * 4, bytes_accessed=rows * feats * 2, transcendentals=0
    )

    bins, low, stats, far_other = pl.pallas_call(
        functools.partial(first_kernel, bits, share),
        out_shape=(
            jax.ShapeDtypeStruct((feats, rows), F32),
            jax.ShapeDtypeStruct((feats, rows), F32),
            jax.ShapeDtypeStruct((STATS, rows), BF16),
            part,
        ),
        in_specs=[HBM] * 5,
        out_specs=(VMEM,) * 4,
        scratch_shapes=[
            pltpu.VMEM((rows, feats), jnp.int32),
            pltpu.VMEM(small, jnp.int32),
            pltpu.VMEM(small, jnp.int32),
            pltpu.VMEM(small, BF16),
            pltpu.VMEM(small, BF16),
            pltpu.SemaphoreType.DMA((5,)),
        ],
        compiler_params=ROOM,
        cost_estimate=cost,
        name="stats_and_far_other",
    )(bin_values, *(x.reshape(small) for x in (leaf_ids, treated, gradient, hessian)))

    def left_sums(far, other, after):
        return pl.pallas_call(
            functools.partial(next_kernel, far, other, bits, share),
            out_shape=part,
            in_specs=[VMEM] * 3 + [ANY],
            out_specs=VMEM,
            compiler_params=ROOM,
            cost_estimate=cost,
            name=("near_", "far_")[far] + ("own", "other")[other],
        )(bins, low, stats, after)

    def swap(x, bit):
        return lax.ppermute(x, "row", [(i, i ^ bit) for i in range(ring)])

    far_core = swap(far_other, 1)
    far = left_sums(1, 0, far_other) + far_core
    came = swap(far, 2)
    near_other = left_sums(0, 1, far)
    near_core = swap(near_other, 1)
    kept = left_sums(0, 0, near_other) + near_core
    half = feats // 4
    for stage in range(2, bits):
        half = half // 2
        sent = kept[half:] + came[half:]
        kept = kept[:half] + came[:half]
        came = swap(sent, 1 << stage)

    split_gain, most = pl.pallas_call(
        gain_kernel,
        out_shape=(
            jax.ShapeDtypeStruct((LEAVES, share, BINS), F32),
            jax.ShapeDtypeStruct((devices, BINS), F32),
        ),
        in_specs=[VMEM] * 2,
        out_specs=(VMEM,) * 2,
        name="gains",
    )(kept, came)
    best = lax.all_to_all(most, ("feat", "row"), 0, 0, tiled=True)
    return split_gain, jnp.max(best, axis=0)[:LEAVES]


def solution(mesh):
    in_specs = (P("row", "feat"), P("row"), P("row"), P("row"), P("row"))
    out_specs = (P(None, ("feat", "row"), None), P())
    return jax.shard_map(
        functools.partial(body, mesh.size), mesh=mesh, in_specs=in_specs, out_specs=out_specs, check_vma=False
    )
```

time: 59 us -> 50 us (0.85)
  Pallas kernels: 17.8 us -> 11 us
  waiting for transfers between devices: 13 us -> 9.84 us
  starting transfers between devices: 7.62 us -> 8.3 us
    pallas_call x1, Pallas kernels: 8.53 us -> 2.83 us  [body(): pl.pallas_call(functools.partial(first_kernel, bits, share), out_shape=(j...]
    ppermute x4 -> x5, waiting for transfers between devices: 13 us -> 9.84 us  [swap(): return lax.ppermute(x, 'row', [(i, i ^ bit) for i in range(ring)])]
    pallas_call x2 -> x3, Pallas kernels: 7.39 us -> 6.38 us  [left_sums(): pl.pallas_call(functools.partial(next_kernel, far, other, bits, share), o...]
    ppermute x4 -> x5, starting transfers between devices: 7.62 us -> 8.3 us  [swap(): return lax.ppermute(x, 'row', [(i, i ^ bit) for i in range(ring)])]
  transfers between devices with their start and end apart: 4 -> 5, of which waited for: 3 -> 3; matrix products, arithmetic and copies ran while one was open for 0% -> 0% of each run, Pallas kernels for 13% -> 9%
where the time goes in v2:
time: 50 us; the launch traced here: 49.7 us
  blocking collectives  13.8 us (28%)
  Pallas kernels  11 us (22%)
  waiting for transfers between devices  9.84 us (20%)
  starting transfers between devices  8.3 us (17%)
  local copies, waits for them, and re-layouts  4.6 us (9%)
  other arithmetic  1.31 us (3%)
  between operations  0.71 us (1%)
    all_to_all x1, blocking collectives, body(): best = lax.all_to_all(most, ('feat', 'row'), 0, 0, tiled=True)  13.8 us
    ppermute x5, waiting for transfers between devices, swap(): return lax.ppermute(x, 'row', [(i, i ^ bit) for i in range(ring)])  9.84 us
    ppermute x5, starting transfers between devices, swap(): return lax.ppermute(x, 'row', [(i, i ^ bit) for i in range(ring)])  8.3 us
    pallas_call x3, Pallas kernels, left_sums(): pl.pallas_call(functools.partial(next_kernel, far, other, bits, share), o...  6.38 us
    unnamed x12, local copies, waits for them, and re-layouts  4.6 us
    pallas_call x1, Pallas kernels, body(): pl.pallas_call(functools.partial(first_kernel, bits, share), out_shape=(j...  2.83 us
    pallas_call x1, Pallas kernels, body(): pl.pallas_call(gain_kernel, out_shape=(jax.ShapeDtypeStruct((LEAVES, shar...  1.82 us
  transfers between devices with their start and end apart: 5, of which 3 were waited for; matrix products, arithmetic and copies ran while one was open for 0% of the time, Pallas kernels for 9%

profile of v2, /device:TPU:0, one launch (start us, length us, event | category | flops | bytes accessed | tf_op | source)
XLA Modules:
  0.0 49.7 jit_solution(11571589011027461456)
XLA Ops:
  0.6 0.0 copy-start.3
  0.6 0.7 %copy-done.3 = bf16[2048]{0:T(1024)(128)(2,1)S(1)} copy-done((bf16[2048]{0:T(1024)(128)(2,1)S(1)}, bf16[2048]{0:T(1024)(128)(2,1)}, u32[]{:S(2)}) %copy-start.3) | copy-done | bytes 4120
  1.3 0.0 copy-start
  1.3 1.2 %copy-done = s32[2048,128]{1,0:T(8,128)S(1)} copy-done((s32[2048,128]{1,0:T(8,128)S(1)}, s32[2048,128]{1,0:T(8,128)}, u32[]{:S(2)}) %copy-start) | copy-done | bytes 1048600
  2.5 0.0 copy-start.1
  2.5 0.7 %copy-done.1 = s32[2048]{0:T(1024)S(1)} copy-done((s32[2048]{0:T(1024)S(1)}, s32[2048]{0:T(1024)}, u32[]{:S(2)}) %copy-start.1) | copy-done | bytes 8216
  3.2 0.0 copy-start.2
  3.2 0.7 %copy-done.2 = s32[2048]{0:T(1024)S(1)} copy-done((s32[2048]{0:T(1024)S(1)}, s32[2048]{0:T(1024)}, u32[]{:S(2)}) %copy-start.2) | copy-done | bytes 8216
  3.9 0.0 copy-start.4
  3.9 0.7 %copy-done.4 = bf16[2048]{0:T(1024)(128)(2,1)S(1)} copy-done((bf16[2048]{0:T(1024)(128)(2,1)S(1)}, bf16[2048]{0:T(1024)(128)(2,1)}, u32[]{:S(2)}) %copy-start.4) | copy-done | bytes 4120
  4.6 2.8 %stats_and_far_other.1 = (f32[128,2048]{1,0:T(8,128)S(1)}, f32[128,2048]{1,0:T(8,128)S(1)}, bf16[16,2048]{1,0:T(8,128)(2,1)S(1)}, f32[32,16,128]{2,1,0:T(8,128)S(1)}) custom-call(s32[2048,128]{1,0:T(8,128)S(1)} %copy-done, s32[16,128]{1,0:T(8,128)S(1)} %bitcast.8, s32[16,128]{1,0:T(8,128)S(1)} %bitcast.9, bf16[16,128]{1,0:T(8,128)(2,1)S(1)} %bitcast.10, ...), custom_call_target="tpu_custom_call" | custom-call | flops 1073741824 | bytes 524288 | tf_op jit(solution)/shard_map/stats_and_far_other/pallas_call | solution.py:148
  7.5 0.5 %collective-permute-start = (f32[32,16,128]{2,1,0:T(8,128)S(1)}, f32[32,16,128]{2,1,0:T(8,128)S(1)}, u32[]{:S(2)}, u32[]{:S(2)}) collective-permute-start(f32[32,16,128]{2,1,0:T(8,128)S(1)} %get-tuple-element.11.after_ref), channel_id=1, source_target_pairs={{0,1},{1,0},{2,3},{3,2},{4,5},{5,4},{6,7},{7,6},{8,9},{9,8},{10,11... | collective-permute-start | bytes 786440 | tf_op jit(solution)/shard_map/ppermute | solution.py:183
  8.0 2.1 %far_own.1 = f32[32,16,128]{2,1,0:T(8,128)S(1)} custom-call(f32[128,2048]{1,0:T(8,128)S(1)} %get-tuple-element.8.bins_ref, f32[128,2048]{1,0:T(8,128)S(1)} %get-tuple-element.9.low_ref, bf16[16,2048]{1,0:T(8,128)(2,1)S(1)} %get-tuple-element.10.stats_ref, f32[32,16,128]{2,1,0:T(8,128)S(1)} %get-tuple-element.11.after_ref), custom_call_target="tpu_custom_call" | custom-call | flops 1073741824 | bytes 524288 | tf_op jit(solution)/shard_map/far_own/pallas_call | solution.py:172
  10.1 0.0 collective-permute-done
  10.2 2.1 %near_other.1.after_ref = f32[32,16,128]{2,1,0:T(8,128)S(1)} custom-call(f32[128,2048]{1,0:T(8,128)S(1)} %get-tuple-element.8.bins_ref, f32[128,2048]{1,0:T(8,128)S(1)} %get-tuple-element.9.low_ref, bf16[16,2048]{1,0:T(8,128)(2,1)S(1)} %get-tuple-element.10.stats_ref, f32[32,16,128]{2,1,0:T(8,128)S(1)} %add.18.after_ref), custom_call_target="tpu_custom_call" | custom-call | flops 1073741824 | bytes 524288 | tf_op jit(solution)/shard_map/near_other/pallas_call | solution.py:172
  12.3 0.1 collective-permute-start.1
  12.4 2.9 %collective-permute-start.2 = (f32[32,16,128]{2,1,0:T(8,128)S(1)}, f32[32,16,128]{2,1,0:T(8,128)S(1)}, u32[]{:S(2)}, u32[]{:S(2)}) collective-permute-start(f32[32,16,128]{2,1,0:T(8,128)S(1)} %add.18.after_ref), channel_id=1, source_target_pairs={{0,2},{1,3},{2,0},{3,1},{4,6},{5,7},{6,4},{7,5},{8,10},{9,11},{10,... | collective-permute-start | bytes 786440 | tf_op jit(solution)/shard_map/ppermute | solution.py:183
  15.4 2.1 %near_own.1 = f32[32,16,128]{2,1,0:T(8,128)S(1)} custom-call(f32[128,2048]{1,0:T(8,128)S(1)} %get-tuple-element.8.bins_ref, f32[128,2048]{1,0:T(8,128)S(1)} %get-tuple-element.9.low_ref, bf16[16,2048]{1,0:T(8,128)(2,1)S(1)} %get-tuple-element.10.stats_ref, f32[32,16,128]{2,1,0:T(8,128)S(1)} %near_other.1.after_ref), custom_call_target="tpu_custom_call" | custom-call | flops 1073741824 | bytes 524288 | tf_op jit(solution)/shard_map/near_own/pallas_call | solution.py:172
  17.5 0.0 collective-permute-done.1
  17.6 4.4 %collective-permute-done.2 = f32[32,16,128]{2,1,0:T(8,128)S(1)} collective-permute-done((f32[32,16,128]{2,1,0:T(8,128)S(1)}, f32[32,16,128]{2,1,0:T(8,128)S(1)}, u32[]{:S(2)}, u32[]{:S(2)}) %collective-permute-start.2) | collective-permute-done | bytes 262176 | tf_op jit(solution)/shard_map/ppermute | solution.py:183
  22.0 1.9 %collective-permute-start.3 = (f32[16,16,128]{2,1,0:T(8,128)S(1)}, f32[16,16,128]{2,1,0:T(8,128)S(1)}, u32[]{:S(2)}, u32[]{:S(2)}) collective-permute-start(f32[16,16,128]{2,1,0:T(8,128)S(1)} %get-tuple-element.15), channel_id=1, source_target_pairs={{0,4},{1,5},{2,6},{3,7},{4,0},{5,1},{6,2},{7,3},{8,12},{9,13},{10,... | collective-permute-start | bytes 393224 | tf_op jit(solution)/shard_map/ppermute | solution.py:183
  23.8 3.1 %collective-permute-done.3 = f32[16,16,128]{2,1,0:T(8,128)S(1)} collective-permute-done((f32[16,16,128]{2,1,0:T(8,128)S(1)}, f32[16,16,128]{2,1,0:T(8,128)S(1)}, u32[]{:S(2)}, u32[]{:S(2)}) %collective-permute-start.3) | collective-permute-done | bytes 131104 | tf_op jit(solution)/shard_map/ppermute | solution.py:183
  27.0 0.6 %slice_add_fusion.2 = (f32[8,16,128]{2,1,0:T(8,128)S(1)}, f32[8,16,128]{2,1,0:T(8,128)}) fusion(f32[16,16,128]{2,1,0:T(8,128)S(1)} %collective-permute-done.3, f32[16,16,128]{2,1,0:T(8,128)S(1)} %get-tuple-element.14), kind=kLoop, calls=%fused_computation.2 | loop fusion | flops 32768 | bytes 393216 | tf_op jit(solution)/shard_map/add | solution.py:194
  27.6 2.8 %collective-permute-start.4 = (f32[8,16,128]{2,1,0:T(8,128)S(1)}, f32[8,16,128]{2,1,0:T(8,128)S(1)}, u32[]{:S(2)}, u32[]{:S(2)}) collective-permute-start(f32[8,16,128]{2,1,0:T(8,128)S(1)} %get-tuple-element.16), channel_id=1, source_target_pairs={{0,8},{1,9},{2,10},{3,11},{4,12},{5,13},{6,14},{7,15},{8,0},{9,1},... | collective-permute-start | bytes 196616 | tf_op jit(solution)/shard_map/ppermute | solution.py:183
  30.5 2.3 %collective-permute-done.4.came_ref = f32[8,16,128]{2,1,0:T(8,128)S(1)} collective-permute-done((f32[8,16,128]{2,1,0:T(8,128)S(1)}, f32[8,16,128]{2,1,0:T(8,128)S(1)}, u32[]{:S(2)}, u32[]{:S(2)}) %collective-permute-start.4) | collective-permute-done | bytes 65568 | tf_op jit(solution)/shard_map/ppermute | solution.py:183
  32.8 0.0 copy-start.5
  32.8 0.6 %copy-done.5 = f32[8,16,128]{2,1,0:T(8,128)} copy-done((f32[8,16,128]{2,1,0:T(8,128)}, f32[8,16,128]{2,1,0:T(8,128)S(1)}, u32[]{:S(2)}) %copy-start.5) | copy-done | bytes 65560
  33.4 1.8 %gains.1 = (f32[4,8,128]{2,1,0:T(8,128)}, f32[32,128]{1,0:T(8,128)}) custom-call(f32[8,16,128]{2,1,0:T(8,128)} %get-tuple-element.17.kept_ref, f32[8,16,128]{2,1,0:T(8,128)} %copy-done.5), custom_call_target="tpu_custom_call" | custom-call | tf_op jit(solution)/shard_map/gains/pallas_call | solution.py:198
  35.3 13.8 %all_to_all.9 = f32[32,1,128]{2,1,0:T(1,128)S(1)} all-to-all(f32[32,1,128]{2,1,0:T(1,128)} %bitcast.12), channel_id=1, replica_groups=mesh['feat'=2,'row'=16] {'feat','row'}, dimensions={0} | all-to-all | bytes 32768 | tf_op jit(solution)/shard_map/all_to_all | solution.py:208
  49.1 0.6 %reduce_max.9 = f32[128]{0:T(128)} reduce(f32[32,1,128]{2,1,0:T(1,128)S(1)} %all_to_all.9, f32[]{:T(128)} %constant.0.clone.1), dimensions={0,1}, to_apply=%region_0.0 | reduce | flops 3968 | bytes 16900 | tf_op jit(solution)/shard_map/reduce_max | solution.py:209
  (3 shorter events, 0.1 us)
Async XLA Ops:
  0.6 0.7 %copy-start.3 = (bf16[2048]{0:T(1024)(128)(2,1)S(1)}, bf16[2048]{0:T(1024)(128)(2,1)}, u32[]{:S(2)}) copy-start(bf16[2048]{0:T(1024)(128)(2,1)} %param.8) | copy-start | bytes 12292
  1.3 1.2 %copy-start = (s32[2048,128]{1,0:T(8,128)S(1)}, s32[2048,128]{1,0:T(8,128)}, u32[]{:S(2)}) copy-start(s32[2048,128]{1,0:T(8,128)} %bins.1) | copy-start | bytes 3145732
  2.5 0.7 %copy-start.1 = (s32[2048]{0:T(1024)S(1)}, s32[2048]{0:T(1024)}, u32[]{:S(2)}) copy-start(s32[2048]{0:T(1024)} %param.6) | copy-start | bytes 24580
  3.2 0.7 %copy-start.2 = (s32[2048]{0:T(1024)S(1)}, s32[2048]{0:T(1024)}, u32[]{:S(2)}) copy-start(s32[2048]{0:T(1024)} %param.7) | copy-start | bytes 24580
  3.9 0.7 %copy-start.4 = (bf16[2048]{0:T(1024)(128)(2,1)S(1)}, bf16[2048]{0:T(1024)(128)(2,1)}, u32[]{:S(2)}) copy-start(bf16[2048]{0:T(1024)(128)(2,1)} %param.9) | copy-start | bytes 12292
  7.5 2.7 %collective-permute-start = (f32[32,16,128]{2,1,0:T(8,128)S(1)}, f32[32,16,128]{2,1,0:T(8,128)S(1)}, u32[]{:S(2)}, u32[]{:S(2)}) collective-permute-start(f32[32,16,128]{2,1,0:T(8,128)S(1)} %get-tuple-element.11.after_ref), channel_id=1, source_target_pairs={{0,1},{1,0},{2,3},{3,2},{4,5},{5,4},{6,7},{7,6},{8,9},{9,8},{10,11... | collective-permute-start | bytes 786440 | tf_op jit(solution)/shard_map/ppermute | solution.py:183
  12.3 5.2 %collective-permute-start.1 = (f32[32,16,128]{2,1,0:T(8,128)S(1)}, f32[32,16,128]{2,1,0:T(8,128)S(1)}, u32[]{:S(2)}, u32[]{:S(2)}) collective-permute-start(f32[32,16,128]{2,1,0:T(8,128)S(1)} %near_other.1.after_ref), channel_id=1, source_target_pairs={{0,1},{1,0},{2,3},{3,2},{4,5},{5,4},{6,7},{7,6},{8,9},{9,8},{10,11... | collective-permute-start | bytes 786440 | tf_op jit(solution)/shard_map/ppermute | solution.py:183
  12.4 9.5 %collective-permute-start.2 = (f32[32,16,128]{2,1,0:T(8,128)S(1)}, f32[32,16,128]{2,1,0:T(8,128)S(1)}, u32[]{:S(2)}, u32[]{:S(2)}) collective-permute-start(f32[32,16,128]{2,1,0:T(8,128)S(1)} %add.18.after_ref), channel_id=1, source_target_pairs={{0,2},{1,3},{2,0},{3,1},{4,6},{5,7},{6,4},{7,5},{8,10},{9,11},{10,... | collective-permute-start | bytes 786440 | tf_op jit(solution)/shard_map/ppermute | solution.py:183
  22.0 5.0 %collective-permute-start.3 = (f32[16,16,128]{2,1,0:T(8,128)S(1)}, f32[16,16,128]{2,1,0:T(8,128)S(1)}, u32[]{:S(2)}, u32[]{:S(2)}) collective-permute-start(f32[16,16,128]{2,1,0:T(8,128)S(1)} %get-tuple-element.15), channel_id=1, source_target_pairs={{0,4},{1,5},{2,6},{3,7},{4,0},{5,1},{6,2},{7,3},{8,12},{9,13},{10,... | collective-permute-start | bytes 393224 | tf_op jit(solution)/shard_map/ppermute | solution.py:183
  27.6 5.2 %collective-permute-start.4 = (f32[8,16,128]{2,1,0:T(8,128)S(1)}, f32[8,16,128]{2,1,0:T(8,128)S(1)}, u32[]{:S(2)}, u32[]{:S(2)}) collective-permute-start(f32[8,16,128]{2,1,0:T(8,128)S(1)} %get-tuple-element.16), channel_id=1, source_target_pairs={{0,8},{1,9},{2,10},{3,11},{4,12},{5,13},{6,14},{7,15},{8,0},{9,1},... | collective-permute-start | bytes 196616 | tf_op jit(solution)/shard_map/ppermute | solution.py:183
  32.8 0.6 %copy-start.5 = (f32[8,16,128]{2,1,0:T(8,128)}, f32[8,16,128]{2,1,0:T(8,128)S(1)}, u32[]{:S(2)}) copy-start(f32[8,16,128]{2,1,0:T(8,128)S(1)} %collective-permute-done.4.came_ref) | copy-start | bytes 196612

commit v3 on v2

v3 whole, which is shorter than its diff:
```python
import functools

import jax
import jax.numpy as jnp
from jax import lax
from jax.experimental import pallas as pl
from jax.experimental.pallas import tpu as pltpu
from jax.sharding import PartitionSpec as P

BINS = 128
LEAVES = 4
STATS = 4 * LEAVES
PACK = 16
HIGH = 4
LOW = BINS // HIGH
GROUP = 8
DEPTH = 256
NT = (((1,), (1,)), ((), ()))
F32, BF16 = jnp.float32, jnp.bfloat16


def reversed_bits(value, bits):
    return sum(((value >> i) & 1) << (bits - 1 - i) for i in range(bits))


def slots_of(bits, fixed, free):
    later = range(1 << (bits - 3))
    return [fixed + free * upper + 8 * reversed_bits(i, bits - 3) for upper in (0, 1) for i in later]


def features_of(bits, share, core, chunk):
    one = [(s, j) for s in slots_of(bits, core + 2 * chunk, 4) for j in range(share // 2)]
    two = [(s, j) for s in slots_of(bits, core + 4 * chunk, 2) for j in range(share // 2, share)]
    return one + two


def stats_of(columns_ref, stats_ref):
    row = lax.broadcasted_iota(jnp.int32, (STATS, 128), 0)
    stat, own_leaf = row // LEAVES, (row % LEAVES).astype(F32)
    blocks = columns_ref.shape[0] // 4
    for i in range(blocks):
        leaf, treated, grad, hess = (
            jnp.broadcast_to(columns_ref[c * blocks + i : c * blocks + i + 1, :], (STATS, 128)) for c in range(4)
        )
        value = jnp.where(stat % 2 == 0, grad, hess)
        ok = (leaf == own_leaf) & ((treated == 1.0) == (stat < 2))
        stats_ref[:, i * 128 : (i + 1) * 128] = jnp.where(ok, value, 0.0).astype(BF16)


def left_sums_of(me, features, share, bins_ref, low_ref, stats_ref, out_ref):
    rows = bins_ref.shape[1]
    steps = lax.broadcasted_iota(jnp.int32, (PACK, DEPTH), 0).astype(F32).astype(BF16)
    one, zero = BF16(1), BF16(0)
    for g in range(out_ref.shape[0] // GROUP):
        feats = [(me ^ slot) * share + j for slot, j in features[g * GROUP : (g + 1) * GROUP]]
        bins = [bins_ref[pl.ds(f, 1), :] for f in feats]
        low = [low_ref[pl.ds(f, 1), :] for f in feats]
        total = jnp.zeros((STATS * (1 + (HIGH - 1) * GROUP), LOW * GROUP), F32)
        for k in range(rows // DEPTH):
            span = slice(k * DEPTH, (k + 1) * DEPTH)
            stats = stats_ref[:, span]
            streamed, ladder = [stats], []
            for j in range(GROUP):
                wide = jnp.broadcast_to(low[j][:, span], (PACK, DEPTH)).astype(BF16)
                for q in range(LOW // PACK):
                    ladder.append(jnp.where(wide <= steps + BF16(PACK * q), one, zero))
                wide = jnp.broadcast_to(bins[j][:, span], (STATS, DEPTH)).astype(BF16)
                for q in range(1, HIGH):
                    streamed.append(jnp.where(wide >= BF16(LOW * q), stats, zero))
            total += lax.dot_general(
                jnp.concatenate(streamed, 0), jnp.concatenate(ladder, 0), NT, preferred_element_type=F32
            )
        for j in range(GROUP):
            columns = slice(LOW * j, LOW * (j + 1))
            reached = [total[:STATS, columns]]
            for q in range(1, HIGH):
                first = STATS * (1 + (HIGH - 1) * j + q - 1)
                reached.append(total[first : first + STATS, columns])
            pieces = []
            for q in range(HIGH):
                piece = reached[q]
                if q + 1 < HIGH:
                    piece = piece - reached[q + 1]
                if q:
                    piece = piece + (reached[0][:, LOW - 1 :] - reached[q][:, LOW - 1 :])
                pieces.append(piece)
            out_ref[g * GROUP + j] = jnp.concatenate(pieces, 1)


def first_kernel(features, share, columns, bins, bins_ref, low_ref, stats_ref, out_ref):
    stats_of(columns, stats_ref)
    turned = bins[...].T
    bins_ref[...] = turned.astype(F32)
    low_ref[...] = (turned % LOW).astype(F32)
    left_sums_of(lax.axis_index("row"), features, share, bins_ref, low_ref, stats_ref, out_ref)


def next_kernel(features, share, bins_ref, low_ref, stats_ref, *refs):
    left_sums_of(lax.axis_index("row"), features, share, bins_ref, low_ref, stats_ref, refs[-1])


def score_of(grad_t, hess_t, grad_c, hess_c):
    value_t = grad_t / (hess_t + 1.0)
    value_c = grad_c / (hess_c + 1.0)
    spread = value_t - value_c
    return grad_t * value_t + grad_c * value_c + (hess_t + hess_c) * spread * spread


def gain_kernel(kept_ref, came_ref, gain_ref, most_ref):
    tops = []
    for leaf in range(LEAVES):
        left = [kept_ref[:, s * LEAVES + leaf, :] + came_ref[:, s * LEAVES + leaf, :] for s in range(4)]
        parent = [jnp.broadcast_to(x[:, BINS - 1 :], x.shape) for x in left]
        right = [p - x for p, x in zip(parent, left)]
        gain = score_of(*left) + score_of(*right) - score_of(*parent)
        gain_ref[leaf] = gain
        tops.append(jnp.max(gain, axis=0, keepdims=True))
    top = jnp.max(jnp.concatenate(tops, 0), axis=1, keepdims=True)
    lane = lax.broadcasted_iota(jnp.int32, (LEAVES, BINS), 1)
    leaf = lax.broadcasted_iota(jnp.int32, (LEAVES, BINS), 0)
    line = jnp.sum(jnp.where(lane == leaf, top, 0.0), axis=0, keepdims=True)
    most_ref[...] = jnp.broadcast_to(line, most_ref.shape)


VMEM = pl.BlockSpec(memory_space=pltpu.VMEM)
ANY = pl.BlockSpec(memory_space=pl.ANY)
ROOM = pltpu.CompilerParams(vmem_limit_bytes=32 * 2**20)


def body(devices, bin_values, leaf_ids, treated, gradient, hessian):
    rows, feats = bin_values.shape
    ring = lax.axis_size("row")
    bits = ring.bit_length() - 1
    share = feats // ring
    part = jax.ShapeDtypeStruct((feats // 4, STATS, BINS), F32)
    cost = pl.CostEstimate(flops=rows * feats, bytes_accessed=rows * feats // 4, transcendentals=0)

    columns = jnp.concatenate([x.astype(F32) for x in (leaf_ids, treated, gradient, hessian)])
    bins, low, stats, other = pl.pallas_call(
        functools.partial(first_kernel, features_of(bits, share, 1, 1), share),
        out_shape=(
            jax.ShapeDtypeStruct((feats, rows), F32),
            jax.ShapeDtypeStruct((feats, rows), F32),
            jax.ShapeDtypeStruct((STATS, rows), BF16),
            part,
        ),
        in_specs=[VMEM] * 2,
        out_specs=(VMEM,) * 4,
        compiler_params=ROOM,
        cost_estimate=cost,
        name="stats_and_first_other",
    )(columns.reshape(4 * rows // 128, 128), bin_values)

    def left_sums(core, chunk, *after):
        return pl.pallas_call(
            functools.partial(next_kernel, features_of(bits, share, core, chunk), share),
            out_shape=part,
            in_specs=[VMEM] * 3 + [ANY] * len(after),
            out_specs=VMEM,
            compiler_params=ROOM,
            cost_estimate=cost,
            name=("second_", "first_")[chunk] + ("own", "other")[core],
        )(bins, low, stats, *after)

    def swap(x, mask):
        return lax.ppermute(x, "row", [(i, i ^ mask) for i in range(ring)])

    def halves(x):
        return x[: x.shape[0] // 2], x[x.shape[0] // 2 :]

    came = swap(other, 1)
    one, two = (x + y for x, y in zip(halves(left_sums(0, 1, other)), halves(came)))
    other = left_sums(1, 0, one, two)
    came_one, came_two = swap(one, 2), swap(two, 4)
    came = swap(other, 1)
    one, two = halves(left_sums(0, 0, other))
    one, two = lax.optimization_barrier((one + came_one, two + came_two))
    came_one, came_two = halves(came)
    (one, far_one), (two, far_two) = ([a + b for a, b in zip(halves(x), halves(y))] for x, y in ((one, came_one), (two, came_two)))
    came_one, came_two = swap(far_one, 4), swap(far_two, 2)

    def joined(one, two):
        pieces = [x.reshape(-1, share // 2, STATS, BINS) for x in (one, two)]
        return jnp.concatenate(pieces, 1).reshape(-1, STATS, BINS)

    kept, came = joined(one, two), joined(came_one, came_two)
    for stage in range(3, bits):
        (kept, sent), (came, came_sent) = halves(kept), halves(came)
        kept, came = kept + came, swap(sent + came_sent, 1 << stage)

    split_gain, most = pl.pallas_call(
        gain_kernel,
        out_shape=(
            jax.ShapeDtypeStruct((LEAVES, share, BINS), F32),
            jax.ShapeDtypeStruct((devices, BINS), F32),
        ),
        in_specs=[VMEM] * 2,
        out_specs=(VMEM,) * 2,
        compiler_params=ROOM,
        name="gains",
    )(kept, came)
    best = lax.all_to_all(most, ("feat", "row"), 0, 0, tiled=True)
    return split_gain, jnp.max(best, axis=0)[:LEAVES]


def solution(mesh):
    in_specs = (P("row", "feat"), P("row"), P("row"), P("row"), P("row"))
    out_specs = (P(None, ("feat", "row"), None), P())
    return jax.shard_map(
        functools.partial(body, mesh.size), mesh=mesh, in_specs=in_specs, out_specs=out_specs, check_vma=False
    )
```

time: 50 us -> 40.2 us (0.80)
  local copies, waits for them, and re-layouts: 4.6 us -> 1.23 us
  blocking collectives: 13.8 us -> 10.5 us
  waiting for transfers between devices: 9.84 us -> 6.99 us
  Pallas kernels: 11 us -> 9.91 us
  starting transfers between devices: 8.3 us -> 9.14 us
    unnamed x12 -> x6, local copies, waits for them, and re-layouts: 4.6 us -> 1.23 us
    all_to_all x1, blocking collectives: 13.8 us -> 10.5 us  [body(): best = lax.all_to_all(most, ('feat', 'row'), 0, 0, tiled=True)]
    ppermute x5 -> x7, waiting for transfers between devices: 9.84 us -> 6.99 us  [swap(): return lax.ppermute(x, 'row', [(i, i ^ mask) for i in range(ring)])]
    pallas_call x1, Pallas kernels: 1.82 us -> 0.88 us  [body(): pl.pallas_call(gain_kernel, out_shape=(jax.ShapeDtypeStruct((LEAVES, shar...]
    ppermute x5 -> x7, starting transfers between devices: 8.3 us -> 9.14 us  [swap(): return lax.ppermute(x, 'row', [(i, i ^ mask) for i in range(ring)])]
    concatenate x0 -> x3, other arithmetic: none -> 0.74 us  [body(): jnp.concatenate([x.astype(F32) for x in (leaf_ids, treated, gradient, hes...]
    add x4, other arithmetic: 0.76 us -> 0.13 us  [the longest x1 0.04 us: body(): a + b]
  transfers between devices with their start and end apart: 5 -> 7, of which waited for: 3 -> 3; matrix products, arithmetic and copies ran while one was open for 0% -> 0% of each run, Pallas kernels for 9% -> 16%
where the time goes in v3:
time: 40.2 us; the launch traced here: 39.9 us
  blocking collectives  10.5 us (26%)
  Pallas kernels  9.91 us (25%)
  starting transfers between devices  9.14 us (23%)
  waiting for transfers between devices  6.99 us (17%)
  other arithmetic  1.42 us (4%)
  local copies, waits for them, and re-layouts  1.23 us (3%)
  between operations  0.76 us (2%)
    all_to_all x1, blocking collectives, body(): best = lax.all_to_all(most, ('feat', 'row'), 0, 0, tiled=True)  10.5 us
    ppermute x7, starting transfers between devices, swap(): return lax.ppermute(x, 'row', [(i, i ^ mask) for i in range(ring)])  9.14 us
    ppermute x7, waiting for transfers between devices, swap(): return lax.ppermute(x, 'row', [(i, i ^ mask) for i in range(ring)])  6.99 us
    pallas_call x3, Pallas kernels, left_sums(): pl.pallas_call(functools.partial(next_kernel, features_of(bits, share, co...  6.39 us
    pallas_call x1, Pallas kernels, body(): pl.pallas_call(functools.partial(first_kernel, features_of(bits, share, 1...  2.64 us
    unnamed x6, local copies, waits for them, and re-layouts  1.23 us
    pallas_call x1, Pallas kernels, body(): pl.pallas_call(gain_kernel, out_shape=(jax.ShapeDtypeStruct((LEAVES, shar...  0.88 us
  transfers between devices with their start and end apart: 7, of which 3 were waited for; matrix products, arithmetic and copies ran while one was open for 0% of the time, Pallas kernels for 16%

profile of v3, /device:TPU:0, one launch (start us, length us, event | category | flops | bytes accessed | tf_op | source)
XLA Modules:
  0.0 39.9 jit_solution(6761240595446384725)
XLA Ops:
  0.6 0.0 copy-start.1
  0.6 0.0 copy-start.2
  0.7 0.7 %convert_bitcast_fusion = (f32[16,128]{1,0:T(8,128)S(1)}, f32[16,128]{1,0:T(8,128)S(1)}) fusion(s32[2048]{0:T(1024)} %param.7, s32[2048]{0:T(1024)} %param.6), kind=kLoop, calls=%fused_computation.21 | loop fusion | flops 4096 | bytes 32768 | tf_op jit(solution)/shard_map/concatenate | solution.py:138
  1.4 0.0 copy-done.1
  1.4 0.0 copy-done.2
  1.4 0.0 copy-start
  1.4 1.2 %copy-done = s32[2048,128]{1,0:T(8,128)S(1)} copy-done((s32[2048,128]{1,0:T(8,128)S(1)}, s32[2048,128]{1,0:T(8,128)}, u32[]{:S(2)}) %copy-start) | copy-done | bytes 1048600
  2.6 2.6 %stats_and_first_other.1 = (f32[128,2048]{1,0:T(8,128)S(1)}, f32[128,2048]{1,0:T(8,128)S(1)}, bf16[16,2048]{1,0:T(8,128)(2,1)S(1)}, f32[32,16,128]{2,1,0:T(8,128)S(1)}) custom-call(f32[64,128]{1,0:T(8,128)S(1)} %pad_maximum_fusion.2.columns, s32[2048,128]{1,0:T(8,128)S(1)} %copy-done), custom_call_target="tpu_custom_call" | custom-call | flops 262144 | bytes 65536 | tf_op jit(solution)/shard_map/stats_and_first_other/pallas_call | solution.py:139
  5.3 0.5 %collective-permute-start = (f32[32,16,128]{2,1,0:T(8,128)S(1)}, f32[32,16,128]{2,1,0:T(8,128)S(1)}, u32[]{:S(2)}, u32[]{:S(2)}) collective-permute-start(f32[32,16,128]{2,1,0:T(8,128)S(1)} %get-tuple-element.13.refs_0_), channel_id=1, source_target_pairs={{0,1},{1,0},{2,3},{3,2},{4,5},{5,4},{6,7},{7,6},{8,9},{9,8},{10,11... | collective-permute-start | bytes 786440 | tf_op jit(solution)/shard_map/ppermute | solution.py:166
  5.8 2.1 %first_own.1 = f32[32,16,128]{2,1,0:T(8,128)S(1)} custom-call(f32[128,2048]{1,0:T(8,128)S(1)} %get-tuple-element.10.bins_ref, f32[128,2048]{1,0:T(8,128)S(1)} %get-tuple-element.11.low_ref, bf16[16,2048]{1,0:T(8,128)(2,1)S(1)} %get-tuple-element.12.stats_ref, f32[32,16,128]{2,1,0:T(8,128)S(1)} %get-tuple-element.13.refs_0_), custom_call_target="tpu_custom_call" | custom-call | flops 262144 | bytes 65536 | tf_op jit(solution)/shard_map/first_own/pallas_call | solution.py:155
  7.9 0.0 collective-permute-done
  8.0 2.6 %collective-permute-start.2 = (f32[16,16,128]{2,1,0:T(8,128)S(1)}, f32[16,16,128]{2,1,0:T(8,128)S(1)}, u32[]{:S(2)}, u32[]{:S(2)}) collective-permute-start(f32[16,16,128]{2,1,0:T(8,128)S(1)} %get-tuple-element.18.refs_1_), channel_id=1, source_target_pairs={{0,4},{1,5},{2,6},{3,7},{4,0},{5,1},{6,2},{7,3},{8,12},{9,13},{10,... | collective-permute-start | bytes 393224 | tf_op jit(solution)/shard_map/ppermute | solution.py:166
  10.6 1.5 %collective-permute-start.1 = (f32[16,16,128]{2,1,0:T(8,128)S(1)}, f32[16,16,128]{2,1,0:T(8,128)S(1)}, u32[]{:S(2)}, u32[]{:S(2)}) collective-permute-start(f32[16,16,128]{2,1,0:T(8,128)S(1)} %get-tuple-element.19.refs_0_), channel_id=1, source_target_pairs={{0,2},{1,3},{2,0},{3,1},{4,6},{5,7},{6,4},{7,5},{8,10},{9,11},{10,... | collective-permute-start | bytes 393224 | tf_op jit(solution)/shard_map/ppermute | solution.py:166
  12.1 2.1 %second_other.1.refs_0_ = f32[32,16,128]{2,1,0:T(8,128)S(1)} custom-call(f32[128,2048]{1,0:T(8,128)S(1)} %get-tuple-element.10.bins_ref, f32[128,2048]{1,0:T(8,128)S(1)} %get-tuple-element.11.low_ref, bf16[16,2048]{1,0:T(8,128)(2,1)S(1)} %get-tuple-element.12.stats_ref, f32[16,16,128]{2,1,0:T(8,128)S(1)} %get-tuple-element.19.refs_0_, ...), custom_call_target="tpu_custom_call" | custom-call | flops 262144 | bytes 65536 | tf_op jit(solution)/shard_map/second_other/pallas_call | solution.py:155
  14.3 0.1 collective-permute-start.3
  14.3 2.1 %second_own.1 = f32[32,16,128]{2,1,0:T(8,128)S(1)} custom-call(f32[128,2048]{1,0:T(8,128)S(1)} %get-tuple-element.10.bins_ref, f32[128,2048]{1,0:T(8,128)S(1)} %get-tuple-element.11.low_ref, bf16[16,2048]{1,0:T(8,128)(2,1)S(1)} %get-tuple-element.12.stats_ref, f32[32,16,128]{2,1,0:T(8,128)S(1)} %second_other.1.refs_0_), custom_call_target="tpu_custom_call" | custom-call | flops 262144 | bytes 65536 | tf_op jit(solution)/shard_map/second_own/pallas_call | solution.py:155
  16.5 0.0 collective-permute-done.2
  16.5 0.0 collective-permute-done.1
  16.6 0.0 collective-permute-done.3
  16.6 1.3 %collective-permute-start.5 = (f32[8,16,128]{2,1,0:T(8,128)S(1)}, f32[8,16,128]{2,1,0:T(8,128)S(1)}, u32[]{:S(2)}, u32[]{:S(2)}) collective-permute-start(f32[8,16,128]{2,1,0:T(8,128)S(1)} %get-tuple-element.21), channel_id=1, source_target_pairs={{0,2},{1,3},{2,0},{3,1},{4,6},{5,7},{6,4},{7,5},{8,10},{9,11},{10,... | collective-permute-start | bytes 196616 | tf_op jit(solution)/shard_map/ppermute | solution.py:166
  17.9 0.5 %collective-permute-start.4 = (f32[8,16,128]{2,1,0:T(8,128)S(1)}, f32[8,16,128]{2,1,0:T(8,128)S(1)}, u32[]{:S(2)}, u32[]{:S(2)}) collective-permute-start(f32[8,16,128]{2,1,0:T(8,128)S(1)} %get-tuple-element.26), channel_id=1, source_target_pairs={{0,4},{1,5},{2,6},{3,7},{4,0},{5,1},{6,2},{7,3},{8,12},{9,13},{10,... | collective-permute-start | bytes 196616 | tf_op jit(solution)/shard_map/ppermute | solution.py:166
  18.4 2.8 %collective-permute-done.5 = f32[8,16,128]{2,1,0:T(8,128)S(1)} collective-permute-done((f32[8,16,128]{2,1,0:T(8,128)S(1)}, f32[8,16,128]{2,1,0:T(8,128)S(1)}, u32[]{:S(2)}, u32[]{:S(2)}) %collective-permute-start.5) | collective-permute-done | bytes 65568 | tf_op jit(solution)/shard_map/ppermute | solution.py:166
  21.2 1.0 %collective-permute-done.4 = f32[8,16,128]{2,1,0:T(8,128)S(1)} collective-permute-done((f32[8,16,128]{2,1,0:T(8,128)S(1)}, f32[8,16,128]{2,1,0:T(8,128)S(1)}, u32[]{:S(2)}, u32[]{:S(2)}) %collective-permute-start.4) | collective-permute-done | bytes 65568 | tf_op jit(solution)/shard_map/ppermute | solution.py:166
  22.2 2.7 %collective-permute-start.6 = (f32[8,16,128]{2,1,0:T(8,128)S(1)}, f32[8,16,128]{2,1,0:T(8,128)S(1)}, u32[]{:S(2)}, u32[]{:S(2)}) collective-permute-start(f32[8,16,128]{2,1,0:T(8,128)S(1)} %get-tuple-element.24), channel_id=1, source_target_pairs={{0,8},{1,9},{2,10},{3,11},{4,12},{5,13},{6,14},{7,15},{8,0},{9,1},... | collective-permute-start | bytes 196616 | tf_op jit(solution)/shard_map/ppermute | solution.py:166
  24.8 3.2 %collective-permute-done.6.came_ref = f32[8,16,128]{2,1,0:T(8,128)S(1)} collective-permute-done((f32[8,16,128]{2,1,0:T(8,128)S(1)}, f32[8,16,128]{2,1,0:T(8,128)S(1)}, u32[]{:S(2)}, u32[]{:S(2)}) %collective-permute-start.6) | collective-permute-done | bytes 65568 | tf_op jit(solution)/shard_map/ppermute | solution.py:166
  28.0 0.9 %gains.1 = (f32[4,8,128]{2,1,0:T(8,128)}, f32[32,128]{1,0:T(8,128)S(1)}) custom-call(f32[8,16,128]{2,1,0:T(8,128)S(1)} %get-tuple-element.25.kept_ref, f32[8,16,128]{2,1,0:T(8,128)S(1)} %collective-permute-done.6.came_ref), custom_call_target="tpu_custom_call" | custom-call | tf_op jit(solution)/shard_map/gains/pallas_call | solution.py:191
  28.9 10.5 %all_to_all.9 = f32[32,1,128]{2,1,0:T(1,128)S(1)} all-to-all(f32[32,1,128]{2,1,0:T(1,128)S(1)} %bitcast.22), channel_id=1, replica_groups=mesh['feat'=2,'row'=16] {'feat','row'}, dimensions={0} | all-to-all | bytes 32768 | tf_op jit(solution)/shard_map/all_to_all | solution.py:202
  39.4 0.6 %reduce_max.9 = f32[128]{0:T(128)} reduce(f32[32,1,128]{2,1,0:T(1,128)S(1)} %all_to_all.9, f32[]{:T(128)} %constant.0.clone.1), dimensions={0,1}, to_apply=%region_0.0 | reduce | flops 3968 | bytes 16900 | tf_op jit(solution)/shard_map/reduce_max | solution.py:203
  (6 shorter events, 0.1 us)
Async XLA Ops:
  0.6 0.8 %copy-start.1 = (bf16[2048]{0:T(1024)(128)(2,1)S(1)}, bf16[2048]{0:T(1024)(128)(2,1)}, u32[]{:S(2)}) copy-start(bf16[2048]{0:T(1024)(128)(2,1)} %param.9) | copy-start | bytes 12292
  0.6 0.7 %copy-start.2 = (bf16[2048]{0:T(1024)(128)(2,1)S(1)}, bf16[2048]{0:T(1024)(128)(2,1)}, u32[]{:S(2)}) copy-start(bf16[2048]{0:T(1024)(128)(2,1)} %param.8) | copy-start | bytes 12292
  1.4 1.2 %copy-start = (s32[2048,128]{1,0:T(8,128)S(1)}, s32[2048,128]{1,0:T(8,128)}, u32[]{:S(2)}) copy-start(s32[2048,128]{1,0:T(8,128)} %bins.1) | copy-start | bytes 3145732
  5.3 2.7 %collective-permute-start = (f32[32,16,128]{2,1,0:T(8,128)S(1)}, f32[32,16,128]{2,1,0:T(8,128)S(1)}, u32[]{:S(2)}, u32[]{:S(2)}) collective-permute-start(f32[32,16,128]{2,1,0:T(8,128)S(1)} %get-tuple-element.13.refs_0_), channel_id=1, source_target_pairs={{0,1},{1,0},{2,3},{3,2},{4,5},{5,4},{6,7},{7,6},{8,9},{9,8},{10,11... | collective-permute-start | bytes 786440 | tf_op jit(solution)/shard_map/ppermute | solution.py:166
  8.0 8.5 %collective-permute-start.2 = (f32[16,16,128]{2,1,0:T(8,128)S(1)}, f32[16,16,128]{2,1,0:T(8,128)S(1)}, u32[]{:S(2)}, u32[]{:S(2)}) collective-permute-start(f32[16,16,128]{2,1,0:T(8,128)S(1)} %get-tuple-element.18.refs_1_), channel_id=1, source_target_pairs={{0,4},{1,5},{2,6},{3,7},{4,0},{5,1},{6,2},{7,3},{8,12},{9,13},{10,... | collective-permute-start | bytes 393224 | tf_op jit(solution)/shard_map/ppermute | solution.py:166
  10.6 5.9 %collective-permute-start.1 = (f32[16,16,128]{2,1,0:T(8,128)S(1)}, f32[16,16,128]{2,1,0:T(8,128)S(1)}, u32[]{:S(2)}, u32[]{:S(2)}) collective-permute-start(f32[16,16,128]{2,1,0:T(8,128)S(1)} %get-tuple-element.19.refs_0_), channel_id=1, source_target_pairs={{0,2},{1,3},{2,0},{3,1},{4,6},{5,7},{6,4},{7,5},{8,10},{9,11},{10,... | collective-permute-start | bytes 393224 | tf_op jit(solution)/shard_map/ppermute | solution.py:166
  14.3 2.3 %collective-permute-start.3 = (f32[32,16,128]{2,1,0:T(8,128)S(1)}, f32[32,16,128]{2,1,0:T(8,128)S(1)}, u32[]{:S(2)}, u32[]{:S(2)}) collective-permute-start(f32[32,16,128]{2,1,0:T(8,128)S(1)} %second_other.1.refs_0_), channel_id=1, source_target_pairs={{0,1},{1,0},{2,3},{3,2},{4,5},{5,4},{6,7},{7,6},{8,9},{9,8},{10,11... | collective-permute-start | bytes 786440 | tf_op jit(solution)/shard_map/ppermute | solution.py:166
  16.6 4.6 %collective-permute-start.5 = (f32[8,16,128]{2,1,0:T(8,128)S(1)}, f32[8,16,128]{2,1,0:T(8,128)S(1)}, u32[]{:S(2)}, u32[]{:S(2)}) collective-permute-start(f32[8,16,128]{2,1,0:T(8,128)S(1)} %get-tuple-element.21), channel_id=1, source_target_pairs={{0,2},{1,3},{2,0},{3,1},{4,6},{5,7},{6,4},{7,5},{8,10},{9,11},{10,... | collective-permute-start | bytes 196616 | tf_op jit(solution)/shard_map/ppermute | solution.py:166
  17.9 4.3 %collective-permute-start.4 = (f32[8,16,128]{2,1,0:T(8,128)S(1)}, f32[8,16,128]{2,1,0:T(8,128)S(1)}, u32[]{:S(2)}, u32[]{:S(2)}) collective-permute-start(f32[8,16,128]{2,1,0:T(8,128)S(1)} %get-tuple-element.26), channel_id=1, source_target_pairs={{0,4},{1,5},{2,6},{3,7},{4,0},{5,1},{6,2},{7,3},{8,12},{9,13},{10,... | collective-permute-start | bytes 196616 | tf_op jit(solution)/shard_map/ppermute | solution.py:166
  22.2 5.8 %collective-permute-start.6 = (f32[8,16,128]{2,1,0:T(8,128)S(1)}, f32[8,16,128]{2,1,0:T(8,128)S(1)}, u32[]{:S(2)}, u32[]{:S(2)}) collective-permute-start(f32[8,16,128]{2,1,0:T(8,128)S(1)} %get-tuple-element.24), channel_id=1, source_target_pairs={{0,8},{1,9},{2,10},{3,11},{4,12},{5,13},{6,14},{7,15},{8,0},{9,1},... | collective-permute-start | bytes 196616 | tf_op jit(solution)/shard_map/ppermute | solution.py:166

commit v4 on v3

--- a/solution.py
+++ b/solution.py
@@ -15,6 +15,7 @@
 LOW = BINS // HIGH
 GROUP = 8
 DEPTH = 256
+BLOCKS = 2
 NT = (((1,), (1,)), ((), ()))
 F32, BF16 = jnp.float32, jnp.bfloat16
 
@@ -23,27 +24,23 @@
     return sum(((value >> i) & 1) << (bits - 1 - i) for i in range(bits))
 
 
-def slots_of(bits, fixed, free):
-    later = range(1 << (bits - 3))
-    return [fixed + free * upper + 8 * reversed_bits(i, bits - 3) for upper in (0, 1) for i in later]
-
-
-def features_of(bits, share, core, chunk):
-    one = [(s, j) for s in slots_of(bits, core + 2 * chunk, 4) for j in range(share // 2)]
-    two = [(s, j) for s in slots_of(bits, core + 4 * chunk, 2) for j in range(share // 2, share)]
-    return one + two
-
-
-def stats_of(columns_ref, stats_ref):
+def features_of(bits, share, core, *nears):
+    out = []
+    for near in nears:
+        slots = [core + 2 * near + 8 * reversed_bits(i, bits - 3) for i in range(1 << (bits - 3))]
+        for half in (range(share // 2), range(share // 2, share)):
+            out += [(s, j) for s in slots for j in half]
+    return out
+
+
+def stats_of(leaf_ref, treated_ref, gradient_ref, hessian_ref, stats_ref):
     row = lax.broadcasted_iota(jnp.int32, (STATS, 128), 0)
-    stat, own_leaf = row // LEAVES, (row % LEAVES).astype(F32)
-    blocks = columns_ref.shape[0] // 4
-    for i in range(blocks):
-        leaf, treated, grad, hess = (
-            jnp.broadcast_to(columns_ref[c * blocks + i : c * blocks + i + 1, :], (STATS, 128)) for c in range(4)
-        )
-        value = jnp.where(stat % 2 == 0, grad, hess)
-        ok = (leaf == own_leaf) & ((treated == 1.0) == (stat < 2))
+    stat, own_leaf = row // LEAVES, row % LEAVES
+    gradient, hessian = gradient_ref[...].astype(F32), hessian_ref[...].astype(F32)
+    for i in range(leaf_ref.shape[0]):
+        wide = lambda x: jnp.broadcast_to(x[i : i + 1, :], (STATS, 128))
+        value = jnp.where(stat % 2 == 0, wide(gradient), wide(hessian))
+        ok = (wide(leaf_ref) == own_leaf) & ((wide(treated_ref) == 1) == (stat < 2))
         stats_ref[:, i * 128 : (i + 1) * 128] = jnp.where(ok, value, 0.0).astype(BF16)
 
 
@@ -81,17 +78,27 @@
                 piece = reached[q]
                 if q + 1 < HIGH:
                     piece = piece - reached[q + 1]
-                if q:
-                    piece = piece + (reached[0][:, LOW - 1 :] - reached[q][:, LOW - 1 :])
                 pieces.append(piece)
             out_ref[g * GROUP + j] = jnp.concatenate(pieces, 1)
 
 
-def first_kernel(features, share, columns, bins, bins_ref, low_ref, stats_ref, out_ref):
-    stats_of(columns, stats_ref)
-    turned = bins[...].T
-    bins_ref[...] = turned.astype(F32)
-    low_ref[...] = (turned % LOW).astype(F32)
+def first_kernel(features, share, bins, leaf, treated, gradient, hessian, bins_ref, low_ref, stats_ref, out_ref, *scratch):
+    columns, held, sems = scratch[:4], scratch[4], scratch[5]
+    small = [
+        pltpu.make_async_copy(src, dst, sems.at[i]) for i, (src, dst) in enumerate(zip((leaf, treated, gradient, hessian), columns))
+    ]
+    blocks = [slice(i, i + held.shape[0] // BLOCKS) for i in range(0, held.shape[0], held.shape[0] // BLOCKS)]
+    large = [pltpu.make_async_copy(bins.at[rows], held.at[rows], sems.at[4 + i]) for i, rows in enumerate(blocks)]
+    for copy in large + small:
+        copy.start()
+    for copy, rows in zip(large, blocks):
+        copy.wait()
+        turned = held[rows].T
+        bins_ref[:, rows] = turned.astype(F32)
+        low_ref[:, rows] = (turned & (LOW - 1)).astype(F32)
+    for copy in small:
+        copy.wait()
+    stats_of(*columns, stats_ref)
     left_sums_of(lax.axis_index("row"), features, share, bins_ref, low_ref, stats_ref, out_ref)
 
 
@@ -106,11 +113,24 @@
     return grad_t * value_t + grad_c * value_c + (hess_t + hess_c) * spread * spread
 
 
-def gain_kernel(kept_ref, came_ref, gain_ref, most_ref):
+def gain_kernel(kept_ref, came_ref, gain_ref, most_ref, sums_ref, parent_ref):
+    share = gain_ref.shape[1]
+    x = (kept_ref[...] + came_ref[...]).reshape(share * STATS, BINS)
+    source = lax.broadcasted_iota(jnp.int32, (BINS, 2 * BINS), 0)
+    target = lax.broadcasted_iota(jnp.int32, (BINS, 2 * BINS), 1)
+    carried = (source % LOW == LOW - 1) & ((target >= BINS) | (source // LOW < target // LOW))
+    carried = jnp.where(carried, 1.0, 0.0).astype(BF16)
+    carry, rest = 0.0, x
+    for _ in range(3):
+        piece = rest.astype(BF16)
+        rest = rest - piece.astype(F32)
+        carry = carry + jnp.dot(piece, carried, preferred_element_type=F32)
+    sums_ref[...] = (x + carry[:, :BINS]).reshape(sums_ref.shape)
+    parent_ref[...] = carry[:, BINS:].reshape(parent_ref.shape)
     tops = []
     for leaf in range(LEAVES):
-        left = [kept_ref[:, s * LEAVES + leaf, :] + came_ref[:, s * LEAVES + leaf, :] for s in range(4)]
-        parent = [jnp.broadcast_to(x[:, BINS - 1 :], x.shape) for x in left]
+        left = [sums_ref[:, s * LEAVES + leaf, :] for s in range(4)]
+        parent = [parent_ref[:, s * LEAVES + leaf, :] for s in range(4)]
         right = [p - x for p, x in zip(parent, left)]
         gain = score_of(*left) + score_of(*right) - score_of(*parent)
         gain_ref[leaf] = gain
@@ -123,6 +143,7 @@
 
 
 VMEM = pl.BlockSpec(memory_space=pltpu.VMEM)
+HBM = pl.BlockSpec(memory_space=pltpu.HBM)
 ANY = pl.BlockSpec(memory_space=pl.ANY)
 ROOM = pltpu.CompilerParams(vmem_limit_bytes=32 * 2**20)
 
@@ -132,34 +153,43 @@
     ring = lax.axis_size("row")
     bits = ring.bit_length() - 1
     share = feats // ring
-    part = jax.ShapeDtypeStruct((feats // 4, STATS, BINS), F32)
+    size = feats // 8
     cost = pl.CostEstimate(flops=rows * feats, bytes_accessed=rows * feats // 4, transcendentals=0)
 
-    columns = jnp.concatenate([x.astype(F32) for x in (leaf_ids, treated, gradient, hessian)])
+    small = (rows // 128, 128)
+    inputs = (bin_values, *(x.reshape(small) for x in (leaf_ids, treated, gradient, hessian)))
     bins, low, stats, other = pl.pallas_call(
-        functools.partial(first_kernel, features_of(bits, share, 1, 1), share),
+        functools.partial(first_kernel, features_of(bits, share, 1, 3), share),
         out_shape=(
             jax.ShapeDtypeStruct((feats, rows), F32),
             jax.ShapeDtypeStruct((feats, rows), F32),
             jax.ShapeDtypeStruct((STATS, rows), BF16),
-            part,
+            jax.ShapeDtypeStruct((size, STATS, BINS), F32),
         ),
-        in_specs=[VMEM] * 2,
+        in_specs=[HBM] * 5,
         out_specs=(VMEM,) * 4,
+        scratch_shapes=[
+            pltpu.VMEM(small, jnp.int32),
+            pltpu.VMEM(small, jnp.int32),
+            pltpu.VMEM(small, BF16),
+            pltpu.VMEM(small, BF16),
+            pltpu.VMEM((rows, feats), jnp.int32),
+            pltpu.SemaphoreType.DMA((4 + BLOCKS,)),
+        ],
         compiler_params=ROOM,
         cost_estimate=cost,
-        name="stats_and_first_other",
-    )(columns.reshape(4 * rows // 128, 128), bin_values)
-
-    def left_sums(core, chunk, *after):
+        name="stats_and_others",
+    )(*(pltpu.with_memory_space_constraint(x, pltpu.HBM) for x in inputs))
+
+    def left_sums(core, nears, *after):
         return pl.pallas_call(
-            functools.partial(next_kernel, features_of(bits, share, core, chunk), share),
-            out_shape=part,
+            functools.partial(next_kernel, features_of(bits, share, core, *nears), share),
+            out_shape=jax.ShapeDtypeStruct((size * len(nears), STATS, BINS), F32),
             in_specs=[VMEM] * 3 + [ANY] * len(after),
             out_specs=VMEM,
             compiler_params=ROOM,
             cost_estimate=cost,
-            name=("second_", "first_")[chunk] + ("own", "other")[core],
+            name="left_sums_%d_%d" % (core, len(nears) * 10 + nears[0]),
         )(bins, low, stats, *after)
 
     def swap(x, mask):
@@ -169,21 +199,25 @@
         return x[: x.shape[0] // 2], x[x.shape[0] // 2 :]
 
     came = swap(other, 1)
-    one, two = (x + y for x, y in zip(halves(left_sums(0, 1, other)), halves(came)))
-    other = left_sums(1, 0, one, two)
+    one, two = (x + y for x, y in zip(halves(left_sums(0, [3], other)), halves(came)))
+    other = left_sums(1, [1, 2], one, two)
+    came_one, came_two = swap(one, 2), swap(two, 4)
+    came = halves(swap(other, 1))
+    along_one, along_two = halves(left_sums(0, [1, 2], other))
+    (one_a, one_b), (two_a, two_b) = halves(along_one), halves(along_two)
+    one_b, two_a = lax.optimization_barrier((one_b + came_two, two_a + came_one))
+    (core_one_a, core_one_b), (core_two_a, core_two_b) = halves(came[0]), halves(came[1])
+    one = jnp.concatenate([one_a + core_one_a, one_b + core_one_b])
+    two = jnp.concatenate([two_a + core_two_a, two_b + core_two_b])
+    other = left_sums(1, [0], one, two)
     came_one, came_two = swap(one, 2), swap(two, 4)
     came = swap(other, 1)
-    one, two = halves(left_sums(0, 0, other))
-    one, two = lax.optimization_barrier((one + came_one, two + came_two))
-    came_one, came_two = halves(came)
-    (one, far_one), (two, far_two) = ([a + b for a, b in zip(halves(x), halves(y))] for x, y in ((one, came_one), (two, came_two)))
-    came_one, came_two = swap(far_one, 4), swap(far_two, 2)
-
-    def joined(one, two):
-        pieces = [x.reshape(-1, share // 2, STATS, BINS) for x in (one, two)]
-        return jnp.concatenate(pieces, 1).reshape(-1, STATS, BINS)
-
-    kept, came = joined(one, two), joined(came_one, came_two)
+    kept = lax.optimization_barrier(left_sums(0, [0], other) + (came_one + came_two))
+
+    def joined(x):
+        return jnp.concatenate([y.reshape(-1, share // 2, STATS, BINS) for y in halves(x)], 1).reshape(-1, STATS, BINS)
+
+    kept, came = joined(kept), joined(came)
     for stage in range(3, bits):
         (kept, sent), (came, came_sent) = halves(kept), halves(came)
         kept, came = kept + came, swap(sent + came_sent, 1 << stage)
@@ -196,6 +230,7 @@
         ),
         in_specs=[VMEM] * 2,
         out_specs=(VMEM,) * 2,
+        scratch_shapes=[pltpu.VMEM((share, STATS, BINS), F32)] * 2,
         compiler_params=ROOM,
         name="gains",
     )(kept, came)

time: 40.2 us -> 38.7 us (0.963)
  local copies, waits for them, and re-layouts: 1.23 us -> 0.02 us
  Pallas kernels: 9.91 us -> 11.1 us
  waiting for transfers between devices: 6.99 us -> 6.04 us
  blocking collectives: 10.5 us -> 11.4 us
  other arithmetic: 1.42 us -> 0.7 us
  starting transfers between devices: 9.14 us -> 8.52 us
    unnamed x6 -> x0, local copies, waits for them, and re-layouts: 1.23 us -> none
    pallas_call x3 -> x5, Pallas kernels: 6.39 us -> 7.37 us  [left_sums(): pl.pallas_call(functools.partial(next_kernel, features_of(bits, share, co...]
    ppermute x7 -> x8, waiting for transfers between devices: 6.99 us -> 6.04 us  [swap(): return lax.ppermute(x, 'row', [(i, i ^ mask) for i in range(ring)])]
    all_to_all x1, blocking collectives: 10.5 us -> 11.4 us  [body(): best = lax.all_to_all(most, ('feat', 'row'), 0, 0, tiled=True)]
    concatenate x3 -> x2, other arithmetic: 0.74 us -> 0.02 us  [the longest x1 0.01 us: body(): one = jnp.concatenate([one_a + core_one_a, one_b + core_one_b])]
    ppermute x7 -> x8, starting transfers between devices: 9.14 us -> 8.52 us  [swap(): return lax.ppermute(x, 'row', [(i, i ^ mask) for i in range(ring)])]
  transfers between devices with their start and end apart: 7 -> 8, of which waited for: 3 -> 3; matrix products, arithmetic and copies ran while one was open for 0% -> 0% of each run, Pallas kernels for 16% -> 19%
where the time goes in v4:
time: 38.7 us; the launch traced here: 38.5 us
  blocking collectives  11.4 us (29%)
  Pallas kernels  11.1 us (29%)
  starting transfers between devices  8.52 us (22%)
  waiting for transfers between devices  6.04 us (16%)
  between operations  0.79 us (2%)
  other arithmetic  0.7 us (2%)
    all_to_all x1, blocking collectives, body(): best = lax.all_to_all(most, ('feat', 'row'), 0, 0, tiled=True)  11.4 us
    ppermute x8, starting transfers between devices, swap(): return lax.ppermute(x, 'row', [(i, i ^ mask) for i in range(ring)])  8.52 us
    pallas_call x5, Pallas kernels, left_sums(): pl.pallas_call(functools.partial(next_kernel, features_of(bits, share, co...  7.37 us
    ppermute x8, waiting for transfers between devices, swap(): return lax.ppermute(x, 'row', [(i, i ^ mask) for i in range(ring)])  6.04 us
    pallas_call x1, Pallas kernels, body(): pl.pallas_call(functools.partial(first_kernel, features_of(bits, share, 1...  2.66 us
    pallas_call x1, Pallas kernels, body(): pl.pallas_call(gain_kernel, out_shape=(jax.ShapeDtypeStruct((LEAVES, shar...  1.03 us
  transfers between devices with their start and end apart: 8, of which 3 were waited for; matrix products, arithmetic and copies ran while one was open for 0% of the time, Pallas kernels for 19%

profile of v4, /device:TPU:0, one launch (start us, length us, event | category | flops | bytes accessed | tf_op | source)
XLA Modules:
  0.0 38.5 jit_solution(15726139938392258792)
XLA Ops:
  0.6 2.7 %stats_and_others.1 = (f32[128,2048]{1,0:T(8,128)S(1)}, f32[128,2048]{1,0:T(8,128)S(1)}, bf16[16,2048]{1,0:T(8,128)(2,1)S(1)}, f32[16,16,128]{2,1,0:T(8,128)S(1)}) custom-call(s32[2048,128]{1,0:T(8,128)} %bins.1, s32[16,128]{1,0:T(8,128)} %bitcast.21, s32[16,128]{1,0:T(8,128)} %bitcast.22, bf16[16,128]{1,0:T(8,128)(2,1)} %bitcast.23, bf16[16,128]{1,0:T(8,128)(2,1)} %bitcast.24), custom_call_target="tpu_custom_call" | custom-call | flops 262144 | bytes 65536 | tf_op jit(solution)/shard_map/stats_and_others/pallas_call | solution.py:161
  3.3 0.5 %collective-permute-start = (f32[16,16,128]{2,1,0:T(8,128)S(1)}, f32[16,16,128]{2,1,0:T(8,128)S(1)}, u32[]{:S(2)}, u32[]{:S(2)}) collective-permute-start(f32[16,16,128]{2,1,0:T(8,128)S(1)} %get-tuple-element.13.refs_0_), channel_id=1, source_target_pairs={{0,1},{1,0},{2,3},{3,2},{4,5},{5,4},{6,7},{7,6},{8,9},{9,8},{10,11... | collective-permute-start | bytes 393224 | tf_op jit(solution)/shard_map/ppermute | solution.py:196
  3.8 1.1 %left_sums_0_13.1 = f32[16,16,128]{2,1,0:T(8,128)S(1)} custom-call(f32[128,2048]{1,0:T(8,128)S(1)} %get-tuple-element.10.bins_ref, f32[128,2048]{1,0:T(8,128)S(1)} %get-tuple-element.11.low_ref, bf16[16,2048]{1,0:T(8,128)(2,1)S(1)} %get-tuple-element.12.stats_ref, f32[16,16,128]{2,1,0:T(8,128)S(1)} %get-tuple-element.13.refs_0_), custom_call_target="tpu_custom_call" | custom-call | flops 262144 | bytes 65536 | tf_op jit(solution)/shard_map/left_sums_0_13/pallas_call | solution.py:185
  5.0 0.0 collective-permute-done
  5.0 2.7 %collective-permute-start.3 = (f32[8,16,128]{2,1,0:T(8,128)S(1)}, f32[8,16,128]{2,1,0:T(8,128)S(1)}, u32[]{:S(2)}, u32[]{:S(2)}) collective-permute-start(f32[8,16,128]{2,1,0:T(8,128)S(1)} %get-tuple-element.26.refs_0_), channel_id=1, source_target_pairs={{0,2},{1,3},{2,0},{3,1},{4,6},{5,7},{6,4},{7,5},{8,10},{9,11},{10,... | collective-permute-start | bytes 196616 | tf_op jit(solution)/shard_map/ppermute | solution.py:196
  7.7 1.6 %collective-permute-start.2 = (f32[8,16,128]{2,1,0:T(8,128)S(1)}, f32[8,16,128]{2,1,0:T(8,128)S(1)}, u32[]{:S(2)}, u32[]{:S(2)}) collective-permute-start(f32[8,16,128]{2,1,0:T(8,128)S(1)} %get-tuple-element.27.refs_1_), channel_id=1, source_target_pairs={{0,4},{1,5},{2,6},{3,7},{4,0},{5,1},{6,2},{7,3},{8,12},{9,13},{10,... | collective-permute-start | bytes 196616 | tf_op jit(solution)/shard_map/ppermute | solution.py:196
  9.3 2.0 %left_sums_1_21.1.refs_0_ = f32[32,16,128]{2,1,0:T(8,128)S(1)} custom-call(f32[128,2048]{1,0:T(8,128)S(1)} %get-tuple-element.10.bins_ref, f32[128,2048]{1,0:T(8,128)S(1)} %get-tuple-element.11.low_ref, bf16[16,2048]{1,0:T(8,128)(2,1)S(1)} %get-tuple-element.12.stats_ref, f32[8,16,128]{2,1,0:T(8,128)S(1)} %get-tuple-element.26.refs_0_, ...), custom_call_target="tpu_custom_call" | custom-call | flops 262144 | bytes 65536 | tf_op jit(solution)/shard_map/left_sums_1_21/pallas_call | solution.py:185
  11.3 0.1 collective-permute-start.1
  11.4 2.0 %left_sums_0_21.1 = f32[32,16,128]{2,1,0:T(8,128)S(1)} custom-call(f32[128,2048]{1,0:T(8,128)S(1)} %get-tuple-element.10.bins_ref, f32[128,2048]{1,0:T(8,128)S(1)} %get-tuple-element.11.low_ref, bf16[16,2048]{1,0:T(8,128)(2,1)S(1)} %get-tuple-element.12.stats_ref, f32[32,16,128]{2,1,0:T(8,128)S(1)} %left_sums_1_21.1.refs_0_), custom_call_target="tpu_custom_call" | custom-call | flops 262144 | bytes 65536 | tf_op jit(solution)/shard_map/left_sums_0_21/pallas_call | solution.py:185
  13.4 0.0 collective-permute-done.3
  13.4 0.0 collective-permute-done.2
  13.4 0.0 collective-permute-done.1
  13.5 0.6 %collective-permute-start.4 = (f32[16,16,128]{2,1,0:T(8,128)S(1)}, f32[16,16,128]{2,1,0:T(8,128)S(1)}, u32[]{:S(2)}, u32[]{:S(2)}) collective-permute-start(f32[16,16,128]{2,1,0:T(8,128)S(1)} %pad_maximum_fusion.refs_0_), channel_id=1, source_target_pairs={{0,2},{1,3},{2,0},{3,1},{4,6},{5,7},{6,4},{7,5},{8,10},{9,11},{10,... | collective-permute-start | bytes 393224 | tf_op jit(solution)/shard_map/ppermute | solution.py:196
  14.1 0.2 collective-permute-start.5
  14.3 1.1 %left_sums_1_10.1.refs_0_ = f32[16,16,128]{2,1,0:T(8,128)S(1)} custom-call(f32[128,2048]{1,0:T(8,128)S(1)} %get-tuple-element.10.bins_ref, f32[128,2048]{1,0:T(8,128)S(1)} %get-tuple-element.11.low_ref, bf16[16,2048]{1,0:T(8,128)(2,1)S(1)} %get-tuple-element.12.stats_ref, f32[16,16,128]{2,1,0:T(8,128)S(1)} %pad_maximum_fusion.refs_0_, ...), custom_call_target="tpu_custom_call" | custom-call | flops 262144 | bytes 65536 | tf_op jit(solution)/shard_map/left_sums_1_10/pallas_call | solution.py:185
  15.5 0.1 collective-permute-start.6
  15.6 1.1 %left_sums_0_10.1 = f32[16,16,128]{2,1,0:T(8,128)S(1)} custom-call(f32[128,2048]{1,0:T(8,128)S(1)} %get-tuple-element.10.bins_ref, f32[128,2048]{1,0:T(8,128)S(1)} %get-tuple-element.11.low_ref, bf16[16,2048]{1,0:T(8,128)(2,1)S(1)} %get-tuple-element.12.stats_ref, f32[16,16,128]{2,1,0:T(8,128)S(1)} %left_sums_1_10.1.refs_0_), custom_call_target="tpu_custom_call" | custom-call | flops 262144 | bytes 65536 | tf_op jit(solution)/shard_map/left_sums_0_10/pallas_call | solution.py:185
  16.8 2.7 %collective-permute-done.4 = f32[16,16,128]{2,1,0:T(8,128)S(1)} collective-permute-done((f32[16,16,128]{2,1,0:T(8,128)S(1)}, f32[16,16,128]{2,1,0:T(8,128)S(1)}, u32[]{:S(2)}, u32[]{:S(2)}) %collective-permute-start.4) | collective-permute-done | bytes 131104 | tf_op jit(solution)/shard_map/ppermute | solution.py:196
  19.5 0.3 collective-permute-done.5
  19.8 0.0 collective-permute-done.6
  19.9 2.7 %collective-permute-start.7 = (f32[8,16,128]{2,1,0:T(8,128)S(1)}, f32[8,16,128]{2,1,0:T(8,128)S(1)}, u32[]{:S(2)}, u32[]{:S(2)}) collective-permute-start(f32[8,16,128]{2,1,0:T(8,128)S(1)} %get-tuple-element.20), channel_id=1, source_target_pairs={{0,8},{1,9},{2,10},{3,11},{4,12},{5,13},{6,14},{7,15},{8,0},{9,1},... | collective-permute-start | bytes 196616 | tf_op jit(solution)/shard_map/ppermute | solution.py:196
  22.5 3.0 %collective-permute-done.7.came_ref = f32[8,16,128]{2,1,0:T(8,128)S(1)} collective-permute-done((f32[8,16,128]{2,1,0:T(8,128)S(1)}, f32[8,16,128]{2,1,0:T(8,128)S(1)}, u32[]{:S(2)}, u32[]{:S(2)}) %collective-permute-start.7) | collective-permute-done | bytes 65568 | tf_op jit(solution)/shard_map/ppermute | solution.py:196
  25.5 1.0 %gains.1 = (f32[4,8,128]{2,1,0:T(8,128)}, f32[32,128]{1,0:T(8,128)S(1)}) custom-call(f32[8,16,128]{2,1,0:T(8,128)S(1)} %get-tuple-element.21.kept_ref, f32[8,16,128]{2,1,0:T(8,128)S(1)} %collective-permute-done.7.came_ref), custom_call_target="tpu_custom_call" | custom-call | tf_op jit(solution)/shard_map/gains/pallas_call | solution.py:225
  26.6 11.4 %all_to_all.9 = f32[32,1,128]{2,1,0:T(1,128)S(1)} all-to-all(f32[32,1,128]{2,1,0:T(1,128)S(1)} %bitcast.16), channel_id=1, replica_groups=mesh['feat'=2,'row'=16] {'feat','row'}, dimensions={0} | all-to-all | bytes 32768 | tf_op jit(solution)/shard_map/all_to_all | solution.py:237
  38.0 0.6 %reduce_max.9 = f32[128]{0:T(128)} reduce(f32[32,1,128]{2,1,0:T(1,128)S(1)} %all_to_all.9, f32[]{:T(128)} %constant.0.clone.1), dimensions={0,1}, to_apply=%region_0.0 | reduce | flops 3968 | bytes 16900 | tf_op jit(solution)/shard_map/reduce_max | solution.py:238
  (9 shorter events, 0.2 us)
Async XLA Ops:
  3.3 1.7 %collective-permute-start = (f32[16,16,128]{2,1,0:T(8,128)S(1)}, f32[16,16,128]{2,1,0:T(8,128)S(1)}, u32[]{:S(2)}, u32[]{:S(2)}) collective-permute-start(f32[16,16,128]{2,1,0:T(8,128)S(1)} %get-tuple-element.13.refs_0_), channel_id=1, source_target_pairs={{0,1},{1,0},{2,3},{3,2},{4,5},{5,4},{6,7},{7,6},{8,9},{9,8},{10,11... | collective-permute-start | bytes 393224 | tf_op jit(solution)/shard_map/ppermute | solution.py:196
  5.0 8.4 %collective-permute-start.3 = (f32[8,16,128]{2,1,0:T(8,128)S(1)}, f32[8,16,128]{2,1,0:T(8,128)S(1)}, u32[]{:S(2)}, u32[]{:S(2)}) collective-permute-start(f32[8,16,128]{2,1,0:T(8,128)S(1)} %get-tuple-element.26.refs_0_), channel_id=1, source_target_pairs={{0,2},{1,3},{2,0},{3,1},{4,6},{5,7},{6,4},{7,5},{8,10},{9,11},{10,... | collective-permute-start | bytes 196616 | tf_op jit(solution)/shard_map/ppermute | solution.py:196
  7.7 5.7 %collective-permute-start.2 = (f32[8,16,128]{2,1,0:T(8,128)S(1)}, f32[8,16,128]{2,1,0:T(8,128)S(1)}, u32[]{:S(2)}, u32[]{:S(2)}) collective-permute-start(f32[8,16,128]{2,1,0:T(8,128)S(1)} %get-tuple-element.27.refs_1_), channel_id=1, source_target_pairs={{0,4},{1,5},{2,6},{3,7},{4,0},{5,1},{6,2},{7,3},{8,12},{9,13},{10,... | collective-permute-start | bytes 196616 | tf_op jit(solution)/shard_map/ppermute | solution.py:196
  11.3 2.1 %collective-permute-start.1 = (f32[32,16,128]{2,1,0:T(8,128)S(1)}, f32[32,16,128]{2,1,0:T(8,128)S(1)}, u32[]{:S(2)}, u32[]{:S(2)}) collective-permute-start(f32[32,16,128]{2,1,0:T(8,128)S(1)} %left_sums_1_21.1.refs_0_), channel_id=1, source_target_pairs={{0,1},{1,0},{2,3},{3,2},{4,5},{5,4},{6,7},{7,6},{8,9},{9,8},{10,11... | collective-permute-start | bytes 786440 | tf_op jit(solution)/shard_map/ppermute | solution.py:196
  13.5 6.0 %collective-permute-start.4 = (f32[16,16,128]{2,1,0:T(8,128)S(1)}, f32[16,16,128]{2,1,0:T(8,128)S(1)}, u32[]{:S(2)}, u32[]{:S(2)}) collective-permute-start(f32[16,16,128]{2,1,0:T(8,128)S(1)} %pad_maximum_fusion.refs_0_), channel_id=1, source_target_pairs={{0,2},{1,3},{2,0},{3,1},{4,6},{5,7},{6,4},{7,5},{8,10},{9,11},{10,... | collective-permute-start | bytes 393224 | tf_op jit(solution)/shard_map/ppermute | solution.py:196
  14.1 5.7 %collective-permute-start.5 = (f32[16,16,128]{2,1,0:T(8,128)S(1)}, f32[16,16,128]{2,1,0:T(8,128)S(1)}, u32[]{:S(2)}, u32[]{:S(2)}) collective-permute-start(f32[16,16,128]{2,1,0:T(8,128)S(1)} %pad_maximum_fusion.1.refs_1_), channel_id=1, source_target_pairs={{0,4},{1,5},{2,6},{3,7},{4,0},{5,1},{6,2},{7,3},{8,12},{9,13},{10,... | collective-permute-start | bytes 393224 | tf_op jit(solution)/shard_map/ppermute | solution.py:196
  15.5 4.3 %collective-permute-start.6 = (f32[16,16,128]{2,1,0:T(8,128)S(1)}, f32[16,16,128]{2,1,0:T(8,128)S(1)}, u32[]{:S(2)}, u32[]{:S(2)}) collective-permute-start(f32[16,16,128]{2,1,0:T(8,128)S(1)} %left_sums_1_10.1.refs_0_), channel_id=1, source_target_pairs={{0,1},{1,0},{2,3},{3,2},{4,5},{5,4},{6,7},{7,6},{8,9},{9,8},{10,11... | collective-permute-start | bytes 393224 | tf_op jit(solution)/shard_map/ppermute | solution.py:196
  19.9 5.7 %collective-permute-start.7 = (f32[8,16,128]{2,1,0:T(8,128)S(1)}, f32[8,16,128]{2,1,0:T(8,128)S(1)}, u32[]{:S(2)}, u32[]{:S(2)}) collective-permute-start(f32[8,16,128]{2,1,0:T(8,128)S(1)} %get-tuple-element.20), channel_id=1, source_target_pairs={{0,8},{1,9},{2,10},{3,11},{4,12},{5,13},{6,14},{7,15},{8,0},{9,1},... | collective-permute-start | bytes 196616 | tf_op jit(solution)/shard_map/ppermute | solution.py:196

commit v5 on v4

--- a/solution.py
+++ b/solution.py
@@ -25,12 +25,8 @@
 
 
 def features_of(bits, share, core, *nears):
-    out = []
-    for near in nears:
-        slots = [core + 2 * near + 8 * reversed_bits(i, bits - 3) for i in range(1 << (bits - 3))]
-        for half in (range(share // 2), range(share // 2, share)):
-            out += [(s, j) for s in slots for j in half]
-    return out
+    slots = [core + 2 * near + 8 * reversed_bits(i, bits - 3) for near in nears for i in range(1 << (bits - 3))]
+    return [(s, j) for s in slots for j in range(share)]
 
 
 def stats_of(leaf_ref, treated_ref, gradient_ref, hessian_ref, stats_ref):
@@ -44,26 +40,27 @@
         stats_ref[:, i * 128 : (i + 1) * 128] = jnp.where(ok, value, 0.0).astype(BF16)
 
 
-def left_sums_of(me, features, share, bins_ref, low_ref, stats_ref, out_ref):
+def left_sums_of(me, features, share, bins_ref, stats_ref, out_ref):
     rows = bins_ref.shape[1]
     steps = lax.broadcasted_iota(jnp.int32, (PACK, DEPTH), 0).astype(F32).astype(BF16)
     one, zero = BF16(1), BF16(0)
     for g in range(out_ref.shape[0] // GROUP):
         feats = [(me ^ slot) * share + j for slot, j in features[g * GROUP : (g + 1) * GROUP]]
         bins = [bins_ref[pl.ds(f, 1), :] for f in feats]
-        low = [low_ref[pl.ds(f, 1), :] for f in feats]
         total = jnp.zeros((STATS * (1 + (HIGH - 1) * GROUP), LOW * GROUP), F32)
         for k in range(rows // DEPTH):
             span = slice(k * DEPTH, (k + 1) * DEPTH)
             stats = stats_ref[:, span]
             streamed, ladder = [stats], []
             for j in range(GROUP):
-                wide = jnp.broadcast_to(low[j][:, span], (PACK, DEPTH)).astype(BF16)
+                wide = jnp.broadcast_to(bins[j][:, span], (STATS, DEPTH)).astype(BF16)
+                low = wide
+                for q in range(1, HIGH):
+                    beyond = wide >= BF16(LOW * q)
+                    streamed.append(jnp.where(beyond, stats, zero))
+                    low = low - jnp.where(beyond, BF16(LOW), zero)
                 for q in range(LOW // PACK):
-                    ladder.append(jnp.where(wide <= steps + BF16(PACK * q), one, zero))
-                wide = jnp.broadcast_to(bins[j][:, span], (STATS, DEPTH)).astype(BF16)
-                for q in range(1, HIGH):
-                    streamed.append(jnp.where(wide >= BF16(LOW * q), stats, zero))
+                    ladder.append(jnp.where(low <= steps + BF16(PACK * q), one, zero))
             total += lax.dot_general(
                 jnp.concatenate(streamed, 0), jnp.concatenate(ladder, 0), NT, preferred_element_type=F32
             )
@@ -82,7 +79,7 @@
             out_ref[g * GROUP + j] = jnp.concatenate(pieces, 1)
 
 
-def first_kernel(features, share, bins, leaf, treated, gradient, hessian, bins_ref, low_ref, stats_ref, out_ref, *scratch):
+def first_kernel(features, share, bins, leaf, treated, gradient, hessian, bins_ref, stats_ref, out_ref, *scratch):
     columns, held, sems = scratch[:4], scratch[4], scratch[5]
     small = [
         pltpu.make_async_copy(src, dst, sems.at[i]) for i, (src, dst) in enumerate(zip((leaf, treated, gradient, hessian), columns))
@@ -95,15 +92,14 @@
         copy.wait()
         turned = held[rows].T
         bins_ref[:, rows] = turned.astype(F32)
-        low_ref[:, rows] = (turned & (LOW - 1)).astype(F32)
     for copy in small:
         copy.wait()
     stats_of(*columns, stats_ref)
-    left_sums_of(lax.axis_index("row"), features, share, bins_ref, low_ref, stats_ref, out_ref)
-
-
-def next_kernel(features, share, bins_ref, low_ref, stats_ref, *refs):
-    left_sums_of(lax.axis_index("row"), features, share, bins_ref, low_ref, stats_ref, refs[-1])
+    left_sums_of(lax.axis_index("row"), features, share, bins_ref, stats_ref, out_ref)
+
+
+def next_kernel(features, share, bins_ref, stats_ref, *refs):
+    left_sums_of(lax.axis_index("row"), features, share, bins_ref, stats_ref, refs[-1])
 
 
 def score_of(grad_t, hess_t, grad_c, hess_c):
@@ -158,16 +154,15 @@
 
     small = (rows // 128, 128)
     inputs = (bin_values, *(x.reshape(small) for x in (leaf_ids, treated, gradient, hessian)))
-    bins, low, stats, other = pl.pallas_call(
+    bins, stats, other = pl.pallas_call(
         functools.partial(first_kernel, features_of(bits, share, 1, 3), share),
         out_shape=(
-            jax.ShapeDtypeStruct((feats, rows), F32),
             jax.ShapeDtypeStruct((feats, rows), F32),
             jax.ShapeDtypeStruct((STATS, rows), BF16),
             jax.ShapeDtypeStruct((size, STATS, BINS), F32),
         ),
         in_specs=[HBM] * 5,
-        out_specs=(VMEM,) * 4,
+        out_specs=(VMEM,) * 3,
         scratch_shapes=[
             pltpu.VMEM(small, jnp.int32),
             pltpu.VMEM(small, jnp.int32),
@@ -185,12 +180,12 @@
         return pl.pallas_call(
             functools.partial(next_kernel, features_of(bits, share, core, *nears), share),
             out_shape=jax.ShapeDtypeStruct((size * len(nears), STATS, BINS), F32),
-            in_specs=[VMEM] * 3 + [ANY] * len(after),
+            in_specs=[VMEM] * 2 + [ANY] * len(after),
             out_specs=VMEM,
             compiler_params=ROOM,
             cost_estimate=cost,
             name="left_sums_%d_%d" % (core, len(nears) * 10 + nears[0]),
-        )(bins, low, stats, *after)
+        )(bins, stats, *after)
 
     def swap(x, mask):
         return lax.ppermute(x, "row", [(i, i ^ mask) for i in range(ring)])
@@ -199,25 +194,16 @@
         return x[: x.shape[0] // 2], x[x.shape[0] // 2 :]
 
     came = swap(other, 1)
-    one, two = (x + y for x, y in zip(halves(left_sums(0, [3], other)), halves(came)))
-    other = left_sums(1, [1, 2], one, two)
-    came_one, came_two = swap(one, 2), swap(two, 4)
+    diagonal = left_sums(0, [3], other) + came
+    other = left_sums(1, [1, 2], diagonal)
+    diagonal = swap(diagonal, 2)
     came = halves(swap(other, 1))
-    along_one, along_two = halves(left_sums(0, [1, 2], other))
-    (one_a, one_b), (two_a, two_b) = halves(along_one), halves(along_two)
-    one_b, two_a = lax.optimization_barrier((one_b + came_two, two_a + came_one))
-    (core_one_a, core_one_b), (core_two_a, core_two_b) = halves(came[0]), halves(came[1])
-    one = jnp.concatenate([one_a + core_one_a, one_b + core_one_b])
-    two = jnp.concatenate([two_a + core_two_a, two_b + core_two_b])
+    one, two = halves(left_sums(0, [1, 2], other))
+    one, two = one + came[0], lax.optimization_barrier(two + diagonal) + came[1]
     other = left_sums(1, [0], one, two)
-    came_one, came_two = swap(one, 2), swap(two, 4)
+    one, two = swap(one, 2), swap(two, 4)
     came = swap(other, 1)
-    kept = lax.optimization_barrier(left_sums(0, [0], other) + (came_one + came_two))
-
-    def joined(x):
-        return jnp.concatenate([y.reshape(-1, share // 2, STATS, BINS) for y in halves(x)], 1).reshape(-1, STATS, BINS)
-
-    kept, came = joined(kept), joined(came)
+    kept = lax.optimization_barrier(left_sums(0, [0], other) + (one + two))
     for stage in range(3, bits):
         (kept, sent), (came, came_sent) = halves(kept), halves(came)
         kept, came = kept + came, swap(sent + came_sent, 1 << stage)

time: 38.7 us -> 38.3 us (0.990)
  waiting for transfers between devices: 6.04 us -> 5.05 us
  starting transfers between devices: 8.52 us -> 9.31 us
    ppermute x8 -> x7, waiting for transfers between devices: 6.04 us -> 5.05 us  [swap(): return lax.ppermute(x, 'row', [(i, i ^ mask) for i in range(ring)])]
    ppermute x8 -> x7, starting transfers between devices: 8.52 us -> 9.31 us  [swap(): return lax.ppermute(x, 'row', [(i, i ^ mask) for i in range(ring)])]
  transfers between devices with their start and end apart: 8 -> 7, of which waited for: 3 -> 3; matrix products, arithmetic and copies ran while one was open for 0% -> 0% of each run, Pallas kernels for 19% -> 20%
where the time goes in v5:
time: 38.3 us; the launch traced here: 38.1 us
  Pallas kernels  11.2 us (29%)
  blocking collectives  11.2 us (29%)
  starting transfers between devices  9.31 us (24%)
  waiting for transfers between devices  5.05 us (13%)
  between operations  0.76 us (2%)
  other arithmetic  0.67 us (2%)
    all_to_all x1, blocking collectives, body(): best = lax.all_to_all(most, ('feat', 'row'), 0, 0, tiled=True)  11.2 us
    ppermute x7, starting transfers between devices, swap(): return lax.ppermute(x, 'row', [(i, i ^ mask) for i in range(ring)])  9.31 us
    pallas_call x5, Pallas kernels, left_sums(): pl.pallas_call(functools.partial(next_kernel, features_of(bits, share, co...  7.45 us
    ppermute x7, waiting for transfers between devices, swap(): return lax.ppermute(x, 'row', [(i, i ^ mask) for i in range(ring)])  5.05 us
    pallas_call x1, Pallas kernels, body(): pl.pallas_call(functools.partial(first_kernel, features_of(bits, share, 1...  2.68 us
    pallas_call x1, Pallas kernels, body(): pl.pallas_call(gain_kernel, out_shape=(jax.ShapeDtypeStruct((LEAVES, shar...  1.03 us
  transfers between devices with their start and end apart: 7, of which 3 were waited for; matrix products, arithmetic and copies ran while one was open for 0% of the time, Pallas kernels for 20%

profile of v5, /device:TPU:0, one launch (start us, length us, event | category | flops | bytes accessed | tf_op | source)
XLA Modules:
  0.0 38.1 jit_solution(18195004396475143606)
XLA Ops:
  0.6 2.7 %stats_and_others.1 = (f32[128,2048]{1,0:T(8,128)S(1)}, bf16[16,2048]{1,0:T(8,128)(2,1)S(1)}, f32[16,16,128]{2,1,0:T(8,128)S(1)}) custom-call(s32[2048,128]{1,0:T(8,128)} %bins.1, s32[16,128]{1,0:T(8,128)} %bitcast.9, s32[16,128]{1,0:T(8,128)} %bitcast.10, bf16[16,128]{1,0:T(8,128)(2,1)} %bitcast.11, bf16[16,128]{1,0:T(8,128)(2,1)} %bitcast.12), custom_call_target="tpu_custom_call" | custom-call | flops 262144 | bytes 65536 | tf_op jit(solution)/shard_map/stats_and_others/pallas_call | solution.py:157
  3.3 0.5 %collective-permute-start = (f32[16,16,128]{2,1,0:T(8,128)S(1)}, f32[16,16,128]{2,1,0:T(8,128)S(1)}, u32[]{:S(2)}, u32[]{:S(2)}) collective-permute-start(f32[16,16,128]{2,1,0:T(8,128)S(1)} %get-tuple-element.9.refs_0_), channel_id=1, source_target_pairs={{0,1},{1,0},{2,3},{3,2},{4,5},{5,4},{6,7},{7,6},{8,9},{9,8},{10,11... | collective-permute-start | bytes 393224 | tf_op jit(solution)/shard_map/ppermute | solution.py:191
  3.8 1.1 %left_sums_0_13.1 = f32[16,16,128]{2,1,0:T(8,128)S(1)} custom-call(f32[128,2048]{1,0:T(8,128)S(1)} %get-tuple-element.7.bins_ref, bf16[16,2048]{1,0:T(8,128)(2,1)S(1)} %get-tuple-element.8.stats_ref, f32[16,16,128]{2,1,0:T(8,128)S(1)} %get-tuple-element.9.refs_0_), custom_call_target="tpu_custom_call" | custom-call | flops 262144 | bytes 65536 | tf_op jit(solution)/shard_map/left_sums_0_13/pallas_call | solution.py:180
  5.0 0.0 collective-permute-done
  5.0 2.7 %collective-permute-start.2 = (f32[16,16,128]{2,1,0:T(8,128)S(1)}, f32[16,16,128]{2,1,0:T(8,128)S(1)}, u32[]{:S(2)}, u32[]{:S(2)}) collective-permute-start(f32[16,16,128]{2,1,0:T(8,128)S(1)} %add.24.refs_0_), channel_id=1, source_target_pairs={{0,2},{1,3},{2,0},{3,1},{4,6},{5,7},{6,4},{7,5},{8,10},{9,11},{10,... | collective-permute-start | bytes 393224 | tf_op jit(solution)/shard_map/ppermute | solution.py:191
  7.8 2.0 %left_sums_1_21.1.refs_0_ = f32[32,16,128]{2,1,0:T(8,128)S(1)} custom-call(f32[128,2048]{1,0:T(8,128)S(1)} %get-tuple-element.7.bins_ref, bf16[16,2048]{1,0:T(8,128)(2,1)S(1)} %get-tuple-element.8.stats_ref, f32[16,16,128]{2,1,0:T(8,128)S(1)} %add.24.refs_0_), custom_call_target="tpu_custom_call" | custom-call | flops 262144 | bytes 65536 | tf_op jit(solution)/shard_map/left_sums_1_21/pallas_call | solution.py:180
  9.8 0.1 collective-permute-start.1
  9.9 2.0 %left_sums_0_21.1 = f32[32,16,128]{2,1,0:T(8,128)S(1)} custom-call(f32[128,2048]{1,0:T(8,128)S(1)} %get-tuple-element.7.bins_ref, bf16[16,2048]{1,0:T(8,128)(2,1)S(1)} %get-tuple-element.8.stats_ref, f32[32,16,128]{2,1,0:T(8,128)S(1)} %left_sums_1_21.1.refs_0_), custom_call_target="tpu_custom_call" | custom-call | flops 262144 | bytes 65536 | tf_op jit(solution)/shard_map/left_sums_0_21/pallas_call | solution.py:180
  11.9 0.0 collective-permute-done.2
  11.9 0.0 collective-permute-done.1
  12.0 1.7 %collective-permute-start.4 = (f32[16,16,128]{2,1,0:T(8,128)S(1)}, f32[16,16,128]{2,1,0:T(8,128)S(1)}, u32[]{:S(2)}, u32[]{:S(2)}) collective-permute-start(f32[16,16,128]{2,1,0:T(8,128)S(1)} %get-tuple-element.14.refs_1_), channel_id=1, source_target_pairs={{0,4},{1,5},{2,6},{3,7},{4,0},{5,1},{6,2},{7,3},{8,12},{9,13},{10,... | collective-permute-start | bytes 393224 | tf_op jit(solution)/shard_map/ppermute | solution.py:191
  13.7 1.5 %collective-permute-start.3 = (f32[16,16,128]{2,1,0:T(8,128)S(1)}, f32[16,16,128]{2,1,0:T(8,128)S(1)}, u32[]{:S(2)}, u32[]{:S(2)}) collective-permute-start(f32[16,16,128]{2,1,0:T(8,128)S(1)} %get-tuple-element.15.refs_0_), channel_id=1, source_target_pairs={{0,2},{1,3},{2,0},{3,1},{4,6},{5,7},{6,4},{7,5},{8,10},{9,11},{10,... | collective-permute-start | bytes 393224 | tf_op jit(solution)/shard_map/ppermute | solution.py:191
  15.2 1.1 %left_sums_1_10.1.refs_0_ = f32[16,16,128]{2,1,0:T(8,128)S(1)} custom-call(f32[128,2048]{1,0:T(8,128)S(1)} %get-tuple-element.7.bins_ref, bf16[16,2048]{1,0:T(8,128)(2,1)S(1)} %get-tuple-element.8.stats_ref, f32[16,16,128]{2,1,0:T(8,128)S(1)} %get-tuple-element.15.refs_0_, f32[16,16,128]{2,1,0:T(8,128)S(1)} %get-tuple-element.14.refs_1_), custom_call_target="tpu_custom_call" | custom-call | flops 262144 | bytes 65536 | tf_op jit(solution)/shard_map/left_sums_1_10/pallas_call | solution.py:180
  16.4 1.1 %left_sums_0_10.1 = f32[16,16,128]{2,1,0:T(8,128)S(1)} custom-call(f32[128,2048]{1,0:T(8,128)S(1)} %get-tuple-element.7.bins_ref, bf16[16,2048]{1,0:T(8,128)(2,1)S(1)} %get-tuple-element.8.stats_ref, f32[16,16,128]{2,1,0:T(8,128)S(1)} %left_sums_1_10.1.refs_0_), custom_call_target="tpu_custom_call" | custom-call | flops 262144 | bytes 65536 | tf_op jit(solution)/shard_map/left_sums_0_10/pallas_call | solution.py:180
  17.5 0.1 collective-permute-start.5
  17.6 0.3 collective-permute-done.4
  17.9 1.3 %collective-permute-done.3 = f32[16,16,128]{2,1,0:T(8,128)S(1)} collective-permute-done((f32[16,16,128]{2,1,0:T(8,128)S(1)}, f32[16,16,128]{2,1,0:T(8,128)S(1)}, u32[]{:S(2)}, u32[]{:S(2)}) %collective-permute-start.3) | collective-permute-done | bytes 131104 | tf_op jit(solution)/shard_map/ppermute | solution.py:191
  19.2 0.0 collective-permute-done.5
  19.3 2.7 %collective-permute-start.6 = (f32[8,16,128]{2,1,0:T(8,128)S(1)}, f32[8,16,128]{2,1,0:T(8,128)S(1)}, u32[]{:S(2)}, u32[]{:S(2)}) collective-permute-start(f32[8,16,128]{2,1,0:T(8,128)S(1)} %get-tuple-element.12), channel_id=1, source_target_pairs={{0,8},{1,9},{2,10},{3,11},{4,12},{5,13},{6,14},{7,15},{8,0},{9,1},... | collective-permute-start | bytes 196616 | tf_op jit(solution)/shard_map/ppermute | solution.py:191
  21.9 3.4 %collective-permute-done.6.came_ref = f32[8,16,128]{2,1,0:T(8,128)S(1)} collective-permute-done((f32[8,16,128]{2,1,0:T(8,128)S(1)}, f32[8,16,128]{2,1,0:T(8,128)S(1)}, u32[]{:S(2)}, u32[]{:S(2)}) %collective-permute-start.6) | collective-permute-done | bytes 65568 | tf_op jit(solution)/shard_map/ppermute | solution.py:191
  25.4 1.0 %gains.1 = (f32[4,8,128]{2,1,0:T(8,128)}, f32[32,128]{1,0:T(8,128)S(1)}) custom-call(f32[8,16,128]{2,1,0:T(8,128)S(1)} %get-tuple-element.13.kept_ref, f32[8,16,128]{2,1,0:T(8,128)S(1)} %collective-permute-done.6.came_ref), custom_call_target="tpu_custom_call" | custom-call | tf_op jit(solution)/shard_map/gains/pallas_call | solution.py:211
  26.4 11.2 %all_to_all.9 = f32[32,1,128]{2,1,0:T(1,128)S(1)} all-to-all(f32[32,1,128]{2,1,0:T(1,128)S(1)} %bitcast.8), channel_id=1, replica_groups=mesh['feat'=2,'row'=16] {'feat','row'}, dimensions={0} | all-to-all | bytes 32768 | tf_op jit(solution)/shard_map/all_to_all | solution.py:223
  37.5 0.6 %reduce_max.9 = f32[128]{0:T(128)} reduce(f32[32,1,128]{2,1,0:T(1,128)S(1)} %all_to_all.9, f32[]{:T(128)} %constant.0.clone.1), dimensions={0,1}, to_apply=%region_0.0 | reduce | flops 3968 | bytes 16900 | tf_op jit(solution)/shard_map/reduce_max | solution.py:224
  (5 shorter events, 0.1 us)
Async XLA Ops:
  3.3 1.7 %collective-permute-start = (f32[16,16,128]{2,1,0:T(8,128)S(1)}, f32[16,16,128]{2,1,0:T(8,128)S(1)}, u32[]{:S(2)}, u32[]{:S(2)}) collective-permute-start(f32[16,16,128]{2,1,0:T(8,128)S(1)} %get-tuple-element.9.refs_0_), channel_id=1, source_target_pairs={{0,1},{1,0},{2,3},{3,2},{4,5},{5,4},{6,7},{7,6},{8,9},{9,8},{10,11... | collective-permute-start | bytes 393224 | tf_op jit(solution)/shard_map/ppermute | solution.py:191
  5.0 6.9 %collective-permute-start.2 = (f32[16,16,128]{2,1,0:T(8,128)S(1)}, f32[16,16,128]{2,1,0:T(8,128)S(1)}, u32[]{:S(2)}, u32[]{:S(2)}) collective-permute-start(f32[16,16,128]{2,1,0:T(8,128)S(1)} %add.24.refs_0_), channel_id=1, source_target_pairs={{0,2},{1,3},{2,0},{3,1},{4,6},{5,7},{6,4},{7,5},{8,10},{9,11},{10,... | collective-permute-start | bytes 393224 | tf_op jit(solution)/shard_map/ppermute | solution.py:191
  9.8 2.2 %collective-permute-start.1 = (f32[32,16,128]{2,1,0:T(8,128)S(1)}, f32[32,16,128]{2,1,0:T(8,128)S(1)}, u32[]{:S(2)}, u32[]{:S(2)}) collective-permute-start(f32[32,16,128]{2,1,0:T(8,128)S(1)} %left_sums_1_21.1.refs_0_), channel_id=1, source_target_pairs={{0,1},{1,0},{2,3},{3,2},{4,5},{5,4},{6,7},{7,6},{8,9},{9,8},{10,11... | collective-permute-start | bytes 786440 | tf_op jit(solution)/shard_map/ppermute | solution.py:191
  12.0 5.9 %collective-permute-start.4 = (f32[16,16,128]{2,1,0:T(8,128)S(1)}, f32[16,16,128]{2,1,0:T(8,128)S(1)}, u32[]{:S(2)}, u32[]{:S(2)}) collective-permute-start(f32[16,16,128]{2,1,0:T(8,128)S(1)} %get-tuple-element.14.refs_1_), channel_id=1, source_target_pairs={{0,4},{1,5},{2,6},{3,7},{4,0},{5,1},{6,2},{7,3},{8,12},{9,13},{10,... | collective-permute-start | bytes 393224 | tf_op jit(solution)/shard_map/ppermute | solution.py:191
  13.7 5.5 %collective-permute-start.3 = (f32[16,16,128]{2,1,0:T(8,128)S(1)}, f32[16,16,128]{2,1,0:T(8,128)S(1)}, u32[]{:S(2)}, u32[]{:S(2)}) collective-permute-start(f32[16,16,128]{2,1,0:T(8,128)S(1)} %get-tuple-element.15.refs_0_), channel_id=1, source_target_pairs={{0,2},{1,3},{2,0},{3,1},{4,6},{5,7},{6,4},{7,5},{8,10},{9,11},{10,... | collective-permute-start | bytes 393224 | tf_op jit(solution)/shard_map/ppermute | solution.py:191
  17.5 1.7 %collective-permute-start.5 = (f32[16,16,128]{2,1,0:T(8,128)S(1)}, f32[16,16,128]{2,1,0:T(8,128)S(1)}, u32[]{:S(2)}, u32[]{:S(2)}) collective-permute-start(f32[16,16,128]{2,1,0:T(8,128)S(1)} %left_sums_1_10.1.refs_0_), channel_id=1, source_target_pairs={{0,1},{1,0},{2,3},{3,2},{4,5},{5,4},{6,7},{7,6},{8,9},{9,8},{10,11... | collective-permute-start | bytes 393224 | tf_op jit(solution)/shard_map/ppermute | solution.py:191
  19.3 6.1 %collective-permute-start.6 = (f32[8,16,128]{2,1,0:T(8,128)S(1)}, f32[8,16,128]{2,1,0:T(8,128)S(1)}, u32[]{:S(2)}, u32[]{:S(2)}) collective-permute-start(f32[8,16,128]{2,1,0:T(8,128)S(1)} %get-tuple-element.12), channel_id=1, source_target_pairs={{0,8},{1,9},{2,10},{3,11},{4,12},{5,13},{6,14},{7,15},{8,0},{9,1},... | collective-permute-start | bytes 196616 | tf_op jit(solution)/shard_map/ppermute | solution.py:191

commit v6 on v5

--- a/solution.py
+++ b/solution.py
@@ -14,7 +14,7 @@
 HIGH = 4
 LOW = BINS // HIGH
 GROUP = 8
-DEPTH = 256
+DEPTH = 512
 BLOCKS = 2
 NT = (((1,), (1,)), ((), ()))
 F32, BF16 = jnp.float32, jnp.bfloat16
@@ -90,8 +90,7 @@
         copy.start()
     for copy, rows in zip(large, blocks):
         copy.wait()
-        turned = held[rows].T
-        bins_ref[:, rows] = turned.astype(F32)
+        bins_ref[:, rows] = held[rows].astype(F32).astype(BF16).T.astype(F32)
     for copy in small:
         copy.wait()
     stats_of(*columns, stats_ref)

time: 38.3 us -> 38.2 us (level)
  no operation moved by 1% of the time
where the time goes in v6:
time: 38.2 us; the launch traced here: 38 us
  blocking collectives  11.2 us (29%)
  Pallas kernels  11 us (29%)
  starting transfers between devices  9.3 us (24%)
  waiting for transfers between devices  5.05 us (13%)
  between operations  0.76 us (2%)
  other arithmetic  0.67 us (2%)
    all_to_all x1, blocking collectives, body(): best = lax.all_to_all(most, ('feat', 'row'), 0, 0, tiled=True)  11.2 us
    ppermute x7, starting transfers between devices, swap(): return lax.ppermute(x, 'row', [(i, i ^ mask) for i in range(ring)])  9.3 us
    pallas_call x5, Pallas kernels, left_sums(): pl.pallas_call(functools.partial(next_kernel, features_of(bits, share, co...  7.46 us
    ppermute x7, waiting for transfers between devices, swap(): return lax.ppermute(x, 'row', [(i, i ^ mask) for i in range(ring)])  5.05 us
    pallas_call x1, Pallas kernels, body(): pl.pallas_call(functools.partial(first_kernel, features_of(bits, share, 1...  2.56 us
    pallas_call x1, Pallas kernels, body(): pl.pallas_call(gain_kernel, out_shape=(jax.ShapeDtypeStruct((LEAVES, shar...  1.03 us
  transfers between devices with their start and end apart: 7, of which 3 were waited for; matrix products, arithmetic and copies ran while one was open for 0% of the time, Pallas kernels for 20%

profile of v6, /device:TPU:0, one launch (start us, length us, event | category | flops | bytes accessed | tf_op | source)
XLA Modules:
  0.0 38.0 jit_solution(17857382574394199254)
XLA Ops:
  0.6 2.6 %stats_and_others.1 = (f32[128,2048]{1,0:T(8,128)S(1)}, bf16[16,2048]{1,0:T(8,128)(2,1)S(1)}, f32[16,16,128]{2,1,0:T(8,128)S(1)}) custom-call(s32[2048,128]{1,0:T(8,128)} %bins.1, s32[16,128]{1,0:T(8,128)} %bitcast.9, s32[16,128]{1,0:T(8,128)} %bitcast.10, bf16[16,128]{1,0:T(8,128)(2,1)} %bitcast.11, bf16[16,128]{1,0:T(8,128)(2,1)} %bitcast.12), custom_call_target="tpu_custom_call" | custom-call | flops 262144 | bytes 65536 | tf_op jit(solution)/shard_map/stats_and_others/pallas_call | solution.py:156
  3.2 0.5 %collective-permute-start = (f32[16,16,128]{2,1,0:T(8,128)S(1)}, f32[16,16,128]{2,1,0:T(8,128)S(1)}, u32[]{:S(2)}, u32[]{:S(2)}) collective-permute-start(f32[16,16,128]{2,1,0:T(8,128)S(1)} %get-tuple-element.9.refs_0_), channel_id=1, source_target_pairs={{0,1},{1,0},{2,3},{3,2},{4,5},{5,4},{6,7},{7,6},{8,9},{9,8},{10,11... | collective-permute-start | bytes 393224 | tf_op jit(solution)/shard_map/ppermute | solution.py:190
  3.7 1.1 %left_sums_0_13.1 = f32[16,16,128]{2,1,0:T(8,128)S(1)} custom-call(f32[128,2048]{1,0:T(8,128)S(1)} %get-tuple-element.7.bins_ref, bf16[16,2048]{1,0:T(8,128)(2,1)S(1)} %get-tuple-element.8.stats_ref, f32[16,16,128]{2,1,0:T(8,128)S(1)} %get-tuple-element.9.refs_0_), custom_call_target="tpu_custom_call" | custom-call | flops 262144 | bytes 65536 | tf_op jit(solution)/shard_map/left_sums_0_13/pallas_call | solution.py:179
  4.9 0.0 collective-permute-done
  4.9 2.7 %collective-permute-start.2 = (f32[16,16,128]{2,1,0:T(8,128)S(1)}, f32[16,16,128]{2,1,0:T(8,128)S(1)}, u32[]{:S(2)}, u32[]{:S(2)}) collective-permute-start(f32[16,16,128]{2,1,0:T(8,128)S(1)} %add.24.refs_0_), channel_id=1, source_target_pairs={{0,2},{1,3},{2,0},{3,1},{4,6},{5,7},{6,4},{7,5},{8,10},{9,11},{10,... | collective-permute-start | bytes 393224 | tf_op jit(solution)/shard_map/ppermute | solution.py:190
  7.6 2.0 %left_sums_1_21.1.refs_0_ = f32[32,16,128]{2,1,0:T(8,128)S(1)} custom-call(f32[128,2048]{1,0:T(8,128)S(1)} %get-tuple-element.7.bins_ref, bf16[16,2048]{1,0:T(8,128)(2,1)S(1)} %get-tuple-element.8.stats_ref, f32[16,16,128]{2,1,0:T(8,128)S(1)} %add.24.refs_0_), custom_call_target="tpu_custom_call" | custom-call | flops 262144 | bytes 65536 | tf_op jit(solution)/shard_map/left_sums_1_21/pallas_call | solution.py:179
  9.6 0.1 collective-permute-start.1
  9.8 2.0 %left_sums_0_21.1 = f32[32,16,128]{2,1,0:T(8,128)S(1)} custom-call(f32[128,2048]{1,0:T(8,128)S(1)} %get-tuple-element.7.bins_ref, bf16[16,2048]{1,0:T(8,128)(2,1)S(1)} %get-tuple-element.8.stats_ref, f32[32,16,128]{2,1,0:T(8,128)S(1)} %left_sums_1_21.1.refs_0_), custom_call_target="tpu_custom_call" | custom-call | flops 262144 | bytes 65536 | tf_op jit(solution)/shard_map/left_sums_0_21/pallas_call | solution.py:179
  11.8 0.0 collective-permute-done.2
  11.8 0.0 collective-permute-done.1
  11.9 1.7 %collective-permute-start.4 = (f32[16,16,128]{2,1,0:T(8,128)S(1)}, f32[16,16,128]{2,1,0:T(8,128)S(1)}, u32[]{:S(2)}, u32[]{:S(2)}) collective-permute-start(f32[16,16,128]{2,1,0:T(8,128)S(1)} %get-tuple-element.14.refs_1_), channel_id=1, source_target_pairs={{0,4},{1,5},{2,6},{3,7},{4,0},{5,1},{6,2},{7,3},{8,12},{9,13},{10,... | collective-permute-start | bytes 393224 | tf_op jit(solution)/shard_map/ppermute | solution.py:190
  13.6 1.5 %collective-permute-start.3 = (f32[16,16,128]{2,1,0:T(8,128)S(1)}, f32[16,16,128]{2,1,0:T(8,128)S(1)}, u32[]{:S(2)}, u32[]{:S(2)}) collective-permute-start(f32[16,16,128]{2,1,0:T(8,128)S(1)} %get-tuple-element.15.refs_0_), channel_id=1, source_target_pairs={{0,2},{1,3},{2,0},{3,1},{4,6},{5,7},{6,4},{7,5},{8,10},{9,11},{10,... | collective-permute-start | bytes 393224 | tf_op jit(solution)/shard_map/ppermute | solution.py:190
  15.1 1.1 %left_sums_1_10.1.refs_0_ = f32[16,16,128]{2,1,0:T(8,128)S(1)} custom-call(f32[128,2048]{1,0:T(8,128)S(1)} %get-tuple-element.7.bins_ref, bf16[16,2048]{1,0:T(8,128)(2,1)S(1)} %get-tuple-element.8.stats_ref, f32[16,16,128]{2,1,0:T(8,128)S(1)} %get-tuple-element.15.refs_0_, f32[16,16,128]{2,1,0:T(8,128)S(1)} %get-tuple-element.14.refs_1_), custom_call_target="tpu_custom_call" | custom-call | flops 262144 | bytes 65536 | tf_op jit(solution)/shard_map/left_sums_1_10/pallas_call | solution.py:179
  16.2 1.2 %left_sums_0_10.1 = f32[16,16,128]{2,1,0:T(8,128)S(1)} custom-call(f32[128,2048]{1,0:T(8,128)S(1)} %get-tuple-element.7.bins_ref, bf16[16,2048]{1,0:T(8,128)(2,1)S(1)} %get-tuple-element.8.stats_ref, f32[16,16,128]{2,1,0:T(8,128)S(1)} %left_sums_1_10.1.refs_0_), custom_call_target="tpu_custom_call" | custom-call | flops 262144 | bytes 65536 | tf_op jit(solution)/shard_map/left_sums_0_10/pallas_call | solution.py:179
  17.4 0.1 collective-permute-start.5
  17.5 0.3 collective-permute-done.4
  17.8 1.3 %collective-permute-done.3 = f32[16,16,128]{2,1,0:T(8,128)S(1)} collective-permute-done((f32[16,16,128]{2,1,0:T(8,128)S(1)}, f32[16,16,128]{2,1,0:T(8,128)S(1)}, u32[]{:S(2)}, u32[]{:S(2)}) %collective-permute-start.3) | collective-permute-done | bytes 131104 | tf_op jit(solution)/shard_map/ppermute | solution.py:190
  19.1 0.0 collective-permute-done.5
  19.2 2.7 %collective-permute-start.6 = (f32[8,16,128]{2,1,0:T(8,128)S(1)}, f32[8,16,128]{2,1,0:T(8,128)S(1)}, u32[]{:S(2)}, u32[]{:S(2)}) collective-permute-start(f32[8,16,128]{2,1,0:T(8,128)S(1)} %get-tuple-element.12), channel_id=1, source_target_pairs={{0,8},{1,9},{2,10},{3,11},{4,12},{5,13},{6,14},{7,15},{8,0},{9,1},... | collective-permute-start | bytes 196616 | tf_op jit(solution)/shard_map/ppermute | solution.py:190
  21.8 3.4 %collective-permute-done.6.came_ref = f32[8,16,128]{2,1,0:T(8,128)S(1)} collective-permute-done((f32[8,16,128]{2,1,0:T(8,128)S(1)}, f32[8,16,128]{2,1,0:T(8,128)S(1)}, u32[]{:S(2)}, u32[]{:S(2)}) %collective-permute-start.6) | collective-permute-done | bytes 65568 | tf_op jit(solution)/shard_map/ppermute | solution.py:190
  25.2 1.0 %gains.1 = (f32[4,8,128]{2,1,0:T(8,128)}, f32[32,128]{1,0:T(8,128)S(1)}) custom-call(f32[8,16,128]{2,1,0:T(8,128)S(1)} %get-tuple-element.13.kept_ref, f32[8,16,128]{2,1,0:T(8,128)S(1)} %collective-permute-done.6.came_ref), custom_call_target="tpu_custom_call" | custom-call | tf_op jit(solution)/shard_map/gains/pallas_call | solution.py:210
  26.3 11.2 %all_to_all.9 = f32[32,1,128]{2,1,0:T(1,128)S(1)} all-to-all(f32[32,1,128]{2,1,0:T(1,128)S(1)} %bitcast.8), channel_id=1, replica_groups=mesh['feat'=2,'row'=16] {'feat','row'}, dimensions={0} | all-to-all | bytes 32768 | tf_op jit(solution)/shard_map/all_to_all | solution.py:222
  37.4 0.6 %reduce_max.9 = f32[128]{0:T(128)} reduce(f32[32,1,128]{2,1,0:T(1,128)S(1)} %all_to_all.9, f32[]{:T(128)} %constant.0.clone.1), dimensions={0,1}, to_apply=%region_0.0 | reduce | flops 3968 | bytes 16900 | tf_op jit(solution)/shard_map/reduce_max | solution.py:223
  (5 shorter events, 0.1 us)
Async XLA Ops:
  3.2 1.7 %collective-permute-start = (f32[16,16,128]{2,1,0:T(8,128)S(1)}, f32[16,16,128]{2,1,0:T(8,128)S(1)}, u32[]{:S(2)}, u32[]{:S(2)}) collective-permute-start(f32[16,16,128]{2,1,0:T(8,128)S(1)} %get-tuple-element.9.refs_0_), channel_id=1, source_target_pairs={{0,1},{1,0},{2,3},{3,2},{4,5},{5,4},{6,7},{7,6},{8,9},{9,8},{10,11... | collective-permute-start | bytes 393224 | tf_op jit(solution)/shard_map/ppermute | solution.py:190
  4.9 6.9 %collective-permute-start.2 = (f32[16,16,128]{2,1,0:T(8,128)S(1)}, f32[16,16,128]{2,1,0:T(8,128)S(1)}, u32[]{:S(2)}, u32[]{:S(2)}) collective-permute-start(f32[16,16,128]{2,1,0:T(8,128)S(1)} %add.24.refs_0_), channel_id=1, source_target_pairs={{0,2},{1,3},{2,0},{3,1},{4,6},{5,7},{6,4},{7,5},{8,10},{9,11},{10,... | collective-permute-start | bytes 393224 | tf_op jit(solution)/shard_map/ppermute | solution.py:190
  9.6 2.2 %collective-permute-start.1 = (f32[32,16,128]{2,1,0:T(8,128)S(1)}, f32[32,16,128]{2,1,0:T(8,128)S(1)}, u32[]{:S(2)}, u32[]{:S(2)}) collective-permute-start(f32[32,16,128]{2,1,0:T(8,128)S(1)} %left_sums_1_21.1.refs_0_), channel_id=1, source_target_pairs={{0,1},{1,0},{2,3},{3,2},{4,5},{5,4},{6,7},{7,6},{8,9},{9,8},{10,11... | collective-permute-start | bytes 786440 | tf_op jit(solution)/shard_map/ppermute | solution.py:190
  11.9 5.9 %collective-permute-start.4 = (f32[16,16,128]{2,1,0:T(8,128)S(1)}, f32[16,16,128]{2,1,0:T(8,128)S(1)}, u32[]{:S(2)}, u32[]{:S(2)}) collective-permute-start(f32[16,16,128]{2,1,0:T(8,128)S(1)} %get-tuple-element.14.refs_1_), channel_id=1, source_target_pairs={{0,4},{1,5},{2,6},{3,7},{4,0},{5,1},{6,2},{7,3},{8,12},{9,13},{10,... | collective-permute-start | bytes 393224 | tf_op jit(solution)/shard_map/ppermute | solution.py:190
  13.6 5.5 %collective-permute-start.3 = (f32[16,16,128]{2,1,0:T(8,128)S(1)}, f32[16,16,128]{2,1,0:T(8,128)S(1)}, u32[]{:S(2)}, u32[]{:S(2)}) collective-permute-start(f32[16,16,128]{2,1,0:T(8,128)S(1)} %get-tuple-element.15.refs_0_), channel_id=1, source_target_pairs={{0,2},{1,3},{2,0},{3,1},{4,6},{5,7},{6,4},{7,5},{8,10},{9,11},{10,... | collective-permute-start | bytes 393224 | tf_op jit(solution)/shard_map/ppermute | solution.py:190
  17.4 1.7 %collective-permute-start.5 = (f32[16,16,128]{2,1,0:T(8,128)S(1)}, f32[16,16,128]{2,1,0:T(8,128)S(1)}, u32[]{:S(2)}, u32[]{:S(2)}) collective-permute-start(f32[16,16,128]{2,1,0:T(8,128)S(1)} %left_sums_1_10.1.refs_0_), channel_id=1, source_target_pairs={{0,1},{1,0},{2,3},{3,2},{4,5},{5,4},{6,7},{7,6},{8,9},{9,8},{10,11... | collective-permute-start | bytes 393224 | tf_op jit(solution)/shard_map/ppermute | solution.py:190
  19.2 6.1 %collective-permute-start.6 = (f32[8,16,128]{2,1,0:T(8,128)S(1)}, f32[8,16,128]{2,1,0:T(8,128)S(1)}, u32[]{:S(2)}, u32[]{:S(2)}) collective-permute-start(f32[8,16,128]{2,1,0:T(8,128)S(1)} %get-tuple-element.12), channel_id=1, source_target_pairs={{0,8},{1,9},{2,10},{3,11},{4,12},{5,13},{6,14},{7,15},{8,0},{9,1},... | collective-permute-start | bytes 196616 | tf_op jit(solution)/shard_map/ppermute | solution.py:190
